TPU v7x, 32 devices: a whole 2x2x4 slice. The times are simulated.
32 devices in a mesh: rep: 4 (over y, x), exp: 8 (over z, core).
Axes of the slice: x: 2, y: 2, z: 4, core: 2. Of those that a mesh axis runs over, the one named last changes fastest.
Arguments:
- tokens: bfloat16 [32, 576, 768], P(('rep', 'exp')), may hold values from -6 to 6
- segments: int32 [32, 576], P(('rep', 'exp')), may hold values from 0 to 3, never falling along the last dimension, each value on 1 to 288 neighbouring positions
- valid: int32 [32, 576], P(('rep', 'exp')), may hold values 0 or 1
- routes: int32 [32, 576, 2], P(('rep', 'exp')), may hold values from 0 to 31, all different within a row
- priority: int32 [32, 576], P(('rep', 'exp')), may hold values from 0 to 575, each once within a row
- ln1_gain: bfloat16 [768], P(('rep', 'exp')), may hold values from 0.5 to 1.5
- ln1_bias: bfloat16 [768], P(('rep', 'exp')), may hold values from -1.1953125 to 1.1953125
- w_query: bfloat16 [768, 768], P(('rep', 'exp')), may hold values from -0.21875 to 0.21875
- query_bias: bfloat16 [768], P(('rep', 'exp')), may hold values from -1.1953125 to 1.1953125
- w_key: bfloat16 [768, 768], P(('rep', 'exp')), may hold values from -0.21875 to 0.21875
- w_value: bfloat16 [768, 768], P(('rep', 'exp')), may hold values from -0.21875 to 0.21875
- value_bias: bfloat16 [768], P(('rep', 'exp')), may hold values from -1.1953125 to 1.1953125
- w_attn_out: bfloat16 [768, 768], P(('rep', 'exp')), may hold values from -2 to 2
- attn_out_bias: bfloat16 [768], P(('rep', 'exp')), may hold values from -1.1953125 to 1.1953125
- ln2_gain: bfloat16 [768], P(('rep', 'exp')), may hold values from 0.5 to 1.5
- ln2_bias: bfloat16 [768], P(('rep', 'exp')), may hold values from -1.1953125 to 1.1953125
- w_router: bfloat16 [768, 32], P(('rep', 'exp')), may hold values from -0.15625 to 0.15625
- expert_in: bfloat16 [32, 768, 3072], P('exp'), may hold values from -0.21875 to 0.21875
- expert_in_bias: bfloat16 [32, 3072], P('exp'), may hold values from -1.796875 to 1.796875
- expert_out: bfloat16 [32, 3072, 768], P('exp'), may hold values from -1.75 to 1.75
- expert_out_bias: bfloat16 [32, 768], P(None, ('rep', 'exp')), may hold values from -12 to 12
- cotangent: bfloat16 [32, 576, 768], P(('rep', 'exp')), may hold values from -6 to 6
Outputs:
- block_output: bfloat16 [32, 576, 768], P(('rep', 'exp'))
- tokens_grad: float32 [32, 576, 768], P(('rep', 'exp'))
- ln1_gain_grad: float32 [768], P(('rep', 'exp'))
- ln1_bias_grad: float32 [768], P(('rep', 'exp'))
- w_query_grad: float32 [768, 768], P(('rep', 'exp'))
- query_bias_grad: float32 [768], P(('rep', 'exp'))
- w_key_grad: float32 [768, 768], P(('rep', 'exp'))
- w_value_grad: float32 [768, 768], P(('rep', 'exp'))
- value_bias_grad: float32 [768], P(('rep', 'exp'))
- w_attn_out_grad: float32 [768, 768], P(('rep', 'exp'))
- attn_out_bias_grad: float32 [768], P(('rep', 'exp'))
- ln2_gain_grad: float32 [768], P(('rep', 'exp'))
- ln2_bias_grad: float32 [768], P(('rep', 'exp'))
- w_router_grad: float32 [768, 32], P(('rep', 'exp'))
- expert_in_grad: float32 [32, 768, 3072], P('exp', None, 'rep')
- expert_in_bias_grad: float32 [32, 3072], P('exp', 'rep')
- expert_out_grad: float32 [32, 3072, 768], P('exp', 'rep')
- expert_out_bias_grad: float32 [32, 768], P(None, ('rep', 'exp'))
Inputs may be any that keep to these rules, and one draw needn't show every extreme that they name: `segments`: within a row segment numbers never fall; each image holds 1 to 288 patches, one exactly that many. `routes`: the 2 experts of one patch differ from each other; different patches of a row may name the same experts; every expert is named by some patch. `priority`: each row holds every patch index once.
All inputs are finite; a program needn't handle non-finite values. No bound on the sum of `valid` on one device may be relied on, other than what follows from the above.
Results may differ from a plain program's by a relative error of at most 0.015.
Values may be sent and summed in bfloat16 or wider, within the bound.
A program may use at most 320 MiB of HBM per device.

v0:
```python
import jax
import jax.numpy as jnp
from jax import lax
from jax.sharding import PartitionSpec as P

HEADS = 12
EXPERTS = 32


epsilon = 1e-06
masked_score = -1e30


def layer_norm(values, gain, bias):
    center = values - jnp.mean(values, axis=-1, keepdims=True)
    spread = jnp.mean(center * center, axis=-1, keepdims=True)
    return center * lax.rsqrt(spread + epsilon) * gain + bias


def slot_table(row_routes, row_priority, valid_mask, experts, capacity):
    top_count = row_routes.shape[1]
    chosen = row_routes[row_priority]
    seq_expert = jnp.transpose(chosen).reshape(-1)
    seq_token = jnp.tile(row_priority, top_count)
    seq_valid = jnp.tile(valid_mask[row_priority], top_count)
    expert_ids = jnp.arange(experts, dtype=jnp.int32)
    onehot = (seq_expert[:, None] == expert_ids[None, :]).astype(jnp.int32) * seq_valid[:, None]
    before = jnp.cumsum(onehot, axis=0, dtype=jnp.int32) - onehot
    position = jnp.sum(before * onehot, axis=1, dtype=jnp.int32)
    kept_mask = seq_valid * (position < capacity).astype(jnp.int32)
    slot_id = jnp.where(kept_mask > 0, seq_expert * capacity + position, experts * capacity)
    return (seq_token, seq_expert, slot_id, kept_mask)


def attention_probs(query_heads, key_heads, allowed, score_scale, log_total):
    scores = (
        jnp.einsum("qhd,khd->hqk", query_heads, key_heads, preferred_element_type=jnp.float32)
        * score_scale
    )
    masked = jnp.where(allowed[None], scores, masked_score)
    if log_total is None:
        top_score = jnp.max(masked, axis=-1, keepdims=True)
        log_total = top_score + jnp.log(
            jnp.sum(jnp.exp(masked - top_score), axis=-1, keepdims=True)
        )
    return (jnp.exp(masked - log_total), log_total)


def gelu_exact(values):
    return jax.nn.gelu(values, approximate=False)


def body(
    tokens,
    segments,
    valid,
    routes,
    priority,
    ln1_gain,
    ln1_bias,
    w_query,
    query_bias,
    w_key,
    w_value,
    value_bias,
    w_attn_out,
    attn_out_bias,
    ln2_gain,
    ln2_bias,
    w_router,
    expert_in,
    expert_in_bias,
    expert_out,
    expert_out_bias,
    cotangent,
):
    gathered = (
        lax.all_gather(ln1_gain, ("rep", "exp"), axis=0, tiled=True),
        lax.all_gather(ln1_bias, ("rep", "exp"), axis=0, tiled=True),
        lax.all_gather(w_query, ("rep", "exp"), axis=0, tiled=True),
        lax.all_gather(query_bias, ("rep", "exp"), axis=0, tiled=True),
        lax.all_gather(w_key, ("rep", "exp"), axis=0, tiled=True),
        lax.all_gather(w_value, ("rep", "exp"), axis=0, tiled=True),
        lax.all_gather(value_bias, ("rep", "exp"), axis=0, tiled=True),
        lax.all_gather(w_attn_out, ("rep", "exp"), axis=0, tiled=True),
        lax.all_gather(attn_out_bias, ("rep", "exp"), axis=0, tiled=True),
        lax.all_gather(ln2_gain, ("rep", "exp"), axis=0, tiled=True),
        lax.all_gather(ln2_bias, ("rep", "exp"), axis=0, tiled=True),
        lax.all_gather(w_router, ("rep", "exp"), axis=0, tiled=True),
        lax.all_gather(expert_out_bias, ("rep", "exp"), axis=1, tiled=True),
    )
    (
        gain_one,
        bias_one,
        query_weight,
        query_shift,
        key_weight,
        value_weight,
        value_shift,
        proj_weight,
        proj_shift,
        gain_two,
        bias_two,
        router_weight,
        result_shift,
    ) = gathered
    gain_one = gain_one.astype(jnp.float32)
    bias_one = bias_one.astype(jnp.float32)
    gain_two = gain_two.astype(jnp.float32)
    bias_two = bias_two.astype(jnp.float32)
    length = tokens.shape[1]
    feature_dim = tokens.shape[2]
    head_count = HEADS
    head_dim = feature_dim // head_count
    local_blocks = expert_in.shape[0]
    groups = lax.axis_size("exp")
    experts = EXPERTS
    split = local_blocks * groups // experts
    top_count = routes.shape[2]
    capacity = (105 * top_count * length + 100 * experts - 1) // (100 * experts)
    score_scale = head_dim ** (-0.5)
    inputs = tokens[0].astype(jnp.float32)
    row_segments = segments[0]
    row_valid = valid[0]
    positions = jnp.arange(length, dtype=jnp.int32)
    allowed = (row_segments[:, None] == row_segments[None, :]) & (
        (row_valid[None, :] > 0) | (positions[:, None] == positions[None, :])
    )
    normed = layer_norm(inputs, gain_one, bias_one).astype(jnp.bfloat16)
    query_rows = (
        jnp.dot(normed, query_weight, preferred_element_type=jnp.float32)
        + query_shift.astype(jnp.float32)
    ).astype(jnp.bfloat16)
    key_rows = jnp.dot(normed, key_weight, preferred_element_type=jnp.float32).astype(jnp.bfloat16)
    value_rows = (
        jnp.dot(normed, value_weight, preferred_element_type=jnp.float32)
        + value_shift.astype(jnp.float32)
    ).astype(jnp.bfloat16)
    query_heads = query_rows.reshape(length, head_count, head_dim)
    key_heads = key_rows.reshape(length, head_count, head_dim)
    value_heads = value_rows.reshape(length, head_count, head_dim)
    attn_weights, log_total = attention_probs(query_heads, key_heads, allowed, score_scale, None)
    mixed = jnp.einsum(
        "hqk,khd->qhd",
        attn_weights.astype(jnp.bfloat16),
        value_heads,
        preferred_element_type=jnp.float32,
    )
    mixed = mixed.reshape(length, feature_dim).astype(jnp.bfloat16)
    residual = (
        inputs
        + jnp.dot(mixed, proj_weight, preferred_element_type=jnp.float32)
        + proj_shift.astype(jnp.float32)
    )
    normed_two = layer_norm(residual, gain_two, bias_two).astype(jnp.bfloat16)
    logits = jnp.dot(normed_two, router_weight, preferred_element_type=jnp.float32)
    logit_exp = jnp.exp(logits - jnp.max(logits, axis=-1, keepdims=True))
    router_probs = logit_exp / jnp.sum(logit_exp, axis=-1, keepdims=True)
    seq_token, seq_expert, slot_id, kept_mask = slot_table(
        routes[0], priority[0], row_valid, experts, capacity
    )
    kept_float = kept_mask.astype(jnp.float32)
    buffer = (
        jnp.zeros((experts * capacity + 1, feature_dim), jnp.bfloat16)
        .at[slot_id]
        .add(normed_two[seq_token])
    )
    expert_slots = buffer[: experts * capacity].reshape(experts, capacity, feature_dim)
    outgoing = jnp.repeat(expert_slots, split, axis=0).reshape(
        groups, local_blocks, capacity, feature_dim
    )
    received = lax.all_to_all(outgoing, "exp", split_axis=0, concat_axis=0, tiled=True)
    pre_act = (
        jnp.einsum("secd,edf->secf", received, expert_in, preferred_element_type=jnp.float32)
        + expert_in_bias.astype(jnp.float32)[None, :, None, :]
    )
    active = gelu_exact(pre_act).astype(jnp.bfloat16)
    result = jnp.einsum("secf,efd->secd", active, expert_out, preferred_element_type=jnp.float32)
    returned = lax.all_to_all(
        result.astype(jnp.bfloat16), "exp", split_axis=0, concat_axis=0, tiled=True
    )
    summed = jnp.sum(
        returned.reshape(experts, split, capacity, feature_dim).astype(jnp.float32), axis=1
    )
    summed = summed + result_shift.astype(jnp.float32)[:, None, :]
    flat_result = jnp.concatenate(
        [summed.reshape(experts * capacity, feature_dim), jnp.zeros((1, feature_dim), jnp.float32)],
        axis=0,
    )
    picked = flat_result[slot_id]
    gate_values = router_probs[seq_token, seq_expert] * kept_float
    combined = (
        jnp.zeros((length, feature_dim), jnp.float32)
        .at[seq_token]
        .add(gate_values[:, None] * picked)
    )
    output = residual + combined
    upstream = cotangent[0].astype(jnp.float32)
    token_grad = upstream[seq_token]
    gate_grad = jnp.sum(token_grad * picked, axis=1) * kept_float
    slot_terms = (
        jnp.zeros((experts * capacity + 1, feature_dim), jnp.float32)
        .at[slot_id]
        .add(gate_values[:, None] * token_grad)
    )
    slot_terms = slot_terms[: experts * capacity].reshape(experts, capacity, feature_dim)
    shift_grad = jnp.sum(slot_terms, axis=1)
    slot_grad = jnp.repeat(slot_terms.astype(jnp.bfloat16), split, axis=0).reshape(
        groups, local_blocks, capacity, feature_dim
    )
    back_grad = lax.all_to_all(slot_grad, "exp", split_axis=0, concat_axis=0, tiled=True)
    active_grad = jnp.einsum(
        "secd,efd->secf", back_grad, expert_out, preferred_element_type=jnp.float32
    )
    gelu_back = jax.vjp(gelu_exact, pre_act)[1]
    pre_grad = gelu_back(active_grad)[0].astype(jnp.bfloat16)
    slot_input_grad = jnp.einsum(
        "secf,edf->secd", pre_grad, expert_in, preferred_element_type=jnp.float32
    ).astype(jnp.bfloat16)
    sent_back = lax.all_to_all(slot_input_grad, "exp", split_axis=0, concat_axis=0, tiled=True)
    back_sum = jnp.sum(
        sent_back.reshape(experts, split, capacity, feature_dim).astype(jnp.float32), axis=1
    )
    flat_back = jnp.concatenate(
        [
            back_sum.reshape(experts * capacity, feature_dim),
            jnp.zeros((1, feature_dim), jnp.float32),
        ],
        axis=0,
    )
    moe_grad = jnp.zeros((length, feature_dim), jnp.float32).at[seq_token].add(flat_back[slot_id])
    out_w_grad = jnp.einsum("secf,secd->efd", active, back_grad, preferred_element_type=jnp.float32)
    in_w_grad = jnp.einsum("secd,secf->edf", received, pre_grad, preferred_element_type=jnp.float32)
    in_b_grad = jnp.sum(pre_grad, axis=(0, 2), dtype=jnp.float32)
    expert_sums = (
        lax.psum_scatter(
            in_w_grad.astype(jnp.bfloat16), "rep", scatter_dimension=2, tiled=True
        ).astype(jnp.float32),
        lax.psum_scatter(
            in_b_grad.astype(jnp.bfloat16), "rep", scatter_dimension=1, tiled=True
        ).astype(jnp.float32),
        lax.psum_scatter(
            out_w_grad.astype(jnp.bfloat16), "rep", scatter_dimension=1, tiled=True
        ).astype(jnp.float32),
    )
    prob_grad = jnp.zeros((length, experts), jnp.float32).at[seq_token, seq_expert].add(gate_grad)
    logit_grad = (
        router_probs * (prob_grad - jnp.sum(router_probs * prob_grad, axis=-1, keepdims=True))
    ).astype(jnp.bfloat16)
    router_w_grad = jnp.dot(normed_two.T, logit_grad, preferred_element_type=jnp.float32)
    normed_two_grad = moe_grad + jnp.dot(
        logit_grad, router_weight.T, preferred_element_type=jnp.float32
    )
    norm_two_back = jax.vjp(layer_norm, residual, gain_two, bias_two)[1]
    residual_ln_grad, gain_two_grad, bias_two_grad = norm_two_back(normed_two_grad)
    residual_grad = upstream + residual_ln_grad
    branch_grad = residual_grad.astype(jnp.bfloat16)
    proj_w_grad = jnp.dot(mixed.T, branch_grad, preferred_element_type=jnp.float32)
    proj_b_grad = jnp.sum(branch_grad, axis=0, dtype=jnp.float32)
    mixed_grad = jnp.dot(branch_grad, proj_weight.T, preferred_element_type=jnp.float32).astype(
        jnp.bfloat16
    )
    mixed_grad = mixed_grad.reshape(length, head_count, head_dim)
    again_probs = attention_probs(query_heads, key_heads, allowed, score_scale, log_total)[0]
    prob_grads = jnp.einsum(
        "qhd,khd->hqk", mixed_grad, value_heads, preferred_element_type=jnp.float32
    )
    value_grad = jnp.einsum(
        "hqk,qhd->khd",
        again_probs.astype(jnp.bfloat16),
        mixed_grad,
        preferred_element_type=jnp.float32,
    )
    value_grad = value_grad.astype(jnp.bfloat16).reshape(length, feature_dim)
    inner_sum = jnp.sum(again_probs * prob_grads, axis=-1, keepdims=True)
    score_grad = (again_probs * (prob_grads - inner_sum)).astype(jnp.bfloat16)
    query_grad = (
        (
            jnp.einsum("hqk,khd->qhd", score_grad, key_heads, preferred_element_type=jnp.float32)
            * score_scale
        )
        .astype(jnp.bfloat16)
        .reshape(length, feature_dim)
    )
    key_grad = (
        (
            jnp.einsum("hqk,qhd->khd", score_grad, query_heads, preferred_element_type=jnp.float32)
            * score_scale
        )
        .astype(jnp.bfloat16)
        .reshape(length, feature_dim)
    )
    query_w_grad = jnp.dot(normed.T, query_grad, preferred_element_type=jnp.float32)
    query_b_grad = jnp.sum(query_grad, axis=0, dtype=jnp.float32)
    key_w_grad = jnp.dot(normed.T, key_grad, preferred_element_type=jnp.float32)
    value_w_grad = jnp.dot(normed.T, value_grad, preferred_element_type=jnp.float32)
    value_b_grad = jnp.sum(value_grad, axis=0, dtype=jnp.float32)
    normed_grad = jnp.dot(query_grad, query_weight.T, preferred_element_type=jnp.float32)
    normed_grad = normed_grad + jnp.dot(key_grad, key_weight.T, preferred_element_type=jnp.float32)
    normed_grad = normed_grad + jnp.dot(
        value_grad, value_weight.T, preferred_element_type=jnp.float32
    )
    norm_one_back = jax.vjp(layer_norm, inputs, gain_one, bias_one)[1]
    input_ln_grad, gain_one_grad, bias_one_grad = norm_one_back(normed_grad)
    tokens_grad = residual_grad + input_ln_grad
    dense_sums = (
        lax.psum_scatter(gain_one_grad, ("rep", "exp"), scatter_dimension=0, tiled=True),
        lax.psum_scatter(bias_one_grad, ("rep", "exp"), scatter_dimension=0, tiled=True),
        lax.psum_scatter(query_w_grad, ("rep", "exp"), scatter_dimension=0, tiled=True),
        lax.psum_scatter(query_b_grad, ("rep", "exp"), scatter_dimension=0, tiled=True),
        lax.psum_scatter(key_w_grad, ("rep", "exp"), scatter_dimension=0, tiled=True),
        lax.psum_scatter(value_w_grad, ("rep", "exp"), scatter_dimension=0, tiled=True),
        lax.psum_scatter(value_b_grad, ("rep", "exp"), scatter_dimension=0, tiled=True),
        lax.psum_scatter(proj_w_grad, ("rep", "exp"), scatter_dimension=0, tiled=True),
        lax.psum_scatter(proj_b_grad, ("rep", "exp"), scatter_dimension=0, tiled=True),
        lax.psum_scatter(gain_two_grad, ("rep", "exp"), scatter_dimension=0, tiled=True),
        lax.psum_scatter(bias_two_grad, ("rep", "exp"), scatter_dimension=0, tiled=True),
        lax.psum_scatter(router_w_grad, ("rep", "exp"), scatter_dimension=0, tiled=True),
        lax.psum_scatter(shift_grad, ("rep", "exp"), scatter_dimension=1, tiled=True),
    )
    return (
        output.astype(jnp.bfloat16)[None],
        tokens_grad[None],
        dense_sums[0],
        dense_sums[1],
        dense_sums[2],
        dense_sums[3],
        dense_sums[4],
        dense_sums[5],
        dense_sums[6],
        dense_sums[7],
        dense_sums[8],
        dense_sums[9],
        dense_sums[10],
        dense_sums[11],
        expert_sums[0],
        expert_sums[1],
        expert_sums[2],
        dense_sums[12],
    )


def solution(mesh):
    in_specs = (
        P(("rep", "exp"), None, None),
        P(("rep", "exp"), None),
        P(("rep", "exp"), None),
        P(("rep", "exp"), None, None),
        P(("rep", "exp"), None),
        P(("rep", "exp")),
        P(("rep", "exp")),
        P(("rep", "exp"), None),
        P(("rep", "exp")),
        P(("rep", "exp"), None),
        P(("rep", "exp"), None),
        P(("rep", "exp")),
        P(("rep", "exp"), None),
        P(("rep", "exp")),
        P(("rep", "exp")),
        P(("rep", "exp")),
        P(("rep", "exp"), None),
        P("exp", None, None),
        P("exp", None),
        P("exp", None, None),
        P(None, ("rep", "exp")),
        P(("rep", "exp"), None, None),
    )
    out_specs = (
        P(("rep", "exp"), None, None),
        P(("rep", "exp"), None, None),
        P(("rep", "exp")),
        P(("rep", "exp")),
        P(("rep", "exp"), None),
        P(("rep", "exp")),
        P(("rep", "exp"), None),
        P(("rep", "exp"), None),
        P(("rep", "exp")),
        P(("rep", "exp"), None),
        P(("rep", "exp")),
        P(("rep", "exp")),
        P(("rep", "exp")),
        P(("rep", "exp"), None),
        P("exp", None, "rep"),
        P("exp", "rep"),
        P("exp", "rep", None),
        P(None, ("rep", "exp")),
    )
    return jax.shard_map(body, mesh=mesh, in_specs=in_specs, out_specs=out_specs, check_vma=False)
```

profile of v0, /device:TPU:0, one launch (start us, length us, event | category | flops | bytes accessed | tf_op | source)
XLA Modules:
  0.0 1646.3 jit_solution(17366308413505006447)
XLA Ops:
  19.6 42.7 %all-reduce.19 = (bf16[768]{0:T(1024)(128)(2,1)S(1)}, bf16[768]{0:T(1024)(128)(2,1)S(1)}, bf16[768]{0:T(1024)(128)(2,1)S(1)}, bf16[768]{0:T(1024)(128)(2,1)S(1)}...) all-reduce(bf16[768]{0:T(1024)(128)(2,1)S(1)} %dynamic-update-slice, ...), channel_id=1, replica_groups=mesh['rep'=4,'exp'=8] {'rep','exp'}, use_global_device_ids=true, to_apply=%add.4 | all-reduce | flops 5376 | bytes 21504
  77.6 46.9 %all-gather.5.cloned.1.call-done = bf16[768,768]{1,0:T(8,128)(2,1)} async-done(((bf16[24,768]{1,0:T(8,128)(2,1)}), bf16[768,768]{1,0:T(8,128)(2,1)}) %all-gather.5.cloned.1.call-update) | async-done | bytes 1179664 | tf_op jit(solution)/shard_map/all_gather | solution.py:83
  128.1 52.5 %all-gather.9.cloned.1.call-done = bf16[768,768]{1,0:T(8,128)(2,1)} async-done(((bf16[24,768]{1,0:T(8,128)(2,1)}), bf16[768,768]{1,0:T(8,128)(2,1)}) %all-gather.9.cloned.1.call-update) | async-done | bytes 1179664 | tf_op jit(solution)/shard_map/all_gather | solution.py:82
  193.8 9.8 exponential_reduce_fusion
  204.2 10.6 convolution_convert_fusion.1
  214.8 21.9 %all-gather.11.cloned.1.call-done = bf16[768,768]{1,0:T(8,128)(2,1)} async-done(((bf16[24,768]{1,0:T(8,128)(2,1)}), bf16[768,768]{1,0:T(8,128)(2,1)}) %all-gather.11.cloned.1.call-update) | async-done | bytes 1179664 | tf_op jit(solution)/shard_map/all_gather | solution.py:85
  240.6 21.7 %scatter_custom_fusion = bf16[1217,768]{1,0:T(8,128)(2,1)} fusion(s32[1152]{0:T(1024)S(1)} %get-tuple-element.27, bf16[576,768]{1,0:T(8,128)(2,1)S(1)} %add_convert_fusion, s32[2048]{0:T(1024)S(1)} %pad_clamp_fusion.1, bf16[]{:T(256)} %constant.54.clone.1), kind=kCustom, calls=%fused_computation.103 | custom fusion | flops 884736 | bytes 1869314 | tf_op jit(solution)/shard_map/scatter-add | solution.py:166
  276.9 44.1 %all-to-all-done = bf16[8,4,38,768]{3,1,2,0:T(4,128)(2,1)} async-done(((bf16[8,4,38,768]{3,1,2,0:T(4,128)(2,1)}), bf16[8,4,38,768]{3,1,2,0:T(4,128)(2,1)}, u32[]{:S(2)}, u32[]{:S(2)}) %all-to-all-start) | async-done | bytes 1867808 | tf_op jit(solution)/shard_map/all_to_all | solution.py:172
  321.0 44.8 %fusion.17 = (bf16[8,4,38,3072]{3,2,0,1:T(8,128)(2,1)S(1)}, f32[8,4,38,3072]{3,2,0,1:T(8,128)}, f32[4,8,38,3072]{3,2,1,0:T(8,128)}) fusion(f32[4,3072]{1,0:T(4,128)S(1)} %convert_element_type.208, bf16[4,768,3072]{2,1,0:T(8,128)(2,1)} %param.39, bf16[8,4,38,768]{3,1,2,0:T(4,128)(2,1)} %all-to-all-done), kind=kOutput, calls=%fused_computation.44 | convolution fusion | flops 5984354304 | bytes 58146816 | tf_op jit(solution)/shard_map/secd,edf->secf/dot_general | solution.py:174
  365.9 13.3 convert_bitcast_fusion.2
  386.4 74.1 %all_gather.51 = bf16[32,768]{0,1:T(8,128)(2,1)S(1)} all-gather(bf16[32,24]{0,1:T(8,128)(2,1)S(1)} %copy-done.61), channel_id=1, replica_groups=mesh['rep'=4,'exp'=8] {'rep','exp'}, dimensions={1}, use_global_device_ids=true | all-gather | bytes 50688 | tf_op jit(solution)/shard_map/all_gather | solution.py:90
  473.0 37.4 %all_gather.50 = bf16[768,32]{1,0:T(8,128)(2,1)S(1)} all-gather(bf16[24,32]{1,0:T(8,128)(2,1)S(1)} %copy-done.62), channel_id=1, replica_groups=mesh['rep'=4,'exp'=8] {'rep','exp'}, dimensions={0}, use_global_device_ids=true | all-gather | bytes 50688 | tf_op jit(solution)/shard_map/all_gather | solution.py:89
  554.9 16.6 %scatter_custom_fusion.2 = f32[1217,768]{1,0:T(8,128)} fusion(s32[1152]{0:T(1024)S(1)} %get-tuple-element.27, f32[1152,768]{1,0:T(8,128)} %gather_fusion.4, f32[]{:T(128)} %constant.44.clone.1, f32[1152]{0:T(1024)S(1)} %convert_multiply_fusion.1), kind=kCustom, calls=%fused_computation.62 | custom fusion | flops 1769472 | bytes 7285764 | tf_op jit(solution)/shard_map/scatter-add | solution.py:204
  578.1 46.8 %all_to_all.20 = bf16[8,4,38,768]{3,1,2,0:T(4,128)(2,1)S(1)} all-to-all(bf16[8,4,38,768]{3,1,2,0:T(4,128)(2,1)S(1)} %copy.142), channel_id=1, replica_groups=mesh['rep'=4,'exp'=8] {'exp'}, dimensions={0} | all-to-all | bytes 3735552 | tf_op jit(solution)/shard_map/all_to_all | solution.py:211
  625.0 21.5 %fusion.113 = (bf16[4,3072]{1,0:T(4,128)(2,1)S(1)}, bf16[8,4,38,3072]{3,2,0,1:T(8,128)(2,1)}) fusion(f32[8,4,38,3072]{3,2,0,1:T(8,128)} %get-tuple-element.49, bf16[4,3072,768]{2,1,0:T(8,128)(2,1)} %param.41, bf16[8,4,38,768]{3,1,2,0:T(4,128)(2,1)S(1)} %all_to_all.20, f32[4,8,38,3072]{3,2,1,0:T(8,128)} %get-tuple-element.56, f32[4,3072]{1,0:T(4,128)S(1)} %copy-done.48), kind=kOutput, calls=%fused_computation.191 | convolution fusion | flops 5797564416 | bytes 58171392 | tf_op jit(solution)/shard_map/secd,efd->secf/dot_general | solution.py:212
  647.8 17.1 %bitcast_convert_fusion.1 = bf16[4,768,3072]{2,1,0:T(8,128)(2,1)} fusion(bf16[8,4,38,3072]{3,2,0,1:T(8,128)(2,1)} %get-tuple-element.67, bf16[8,4,38,768]{3,1,2,0:T(4,128)(2,1)} %all-to-all-done), kind=kOutput, calls=%fused_computation.13 | convolution fusion | flops 5747245056 | bytes 28213248 | tf_op jit(solution)/shard_map/secd,secf->edf/dot_general | solution.py:233
  665.2 19.6 %bitcast_convert_fusion = bf16[4,3072,768]{2,1,0:T(8,128)(2,1)} fusion(bf16[8,4,38,3072]{3,2,0,1:T(8,128)(2,1)} %copy-done.78, bf16[8,4,38,768]{3,1,2,0:T(4,128)(2,1)S(1)} %all_to_all.20), kind=kOutput, calls=%fused_computation.12 | convolution fusion | flops 5747245056 | bytes 28213248 | tf_op jit(solution)/shard_map/secf,secd->efd/dot_general | solution.py:232
  684.8 12.8 convert_bitcast_fusion.1
  719.1 29.6 %all-to-all-done.3 = bf16[8,4,38,768]{3,1,2,0:T(4,128)(2,1)} async-done(((bf16[8,4,38,768]{3,1,2,0:T(4,128)(2,1)}), bf16[8,4,38,768]{3,1,2,0:T(4,128)(2,1)}, u32[]{:S(2)}, u32[]{:S(2)}) %all-to-all-start.3) | async-done | bytes 1867808 | tf_op jit(solution)/shard_map/all_to_all | solution.py:220
  759.2 29.7 %scatter_custom_fusion.3 = f32[576,768]{1,0:T(8,128)S(1)} fusion(f32[576,768]{1,0:T(8,128)S(1)} %fusion.114, s32[1152]{0:T(1024)} %copy-done.59, f32[1217,768]{1,0:T(8,128)} %pad_convert_fusion, s32[2048]{0:T(1024)} %copy-done.58), kind=kCustom, calls=%fused_computation.60 | custom fusion | flops 884736 | bytes 1769472 | tf_op jit(solution)/shard_map/scatter-add | solution.py:231
  801.1 11.4 convert_reduce_fusion.1
  816.3 19.1 %multiply_reduce_fusion = (f32[12,576]{1,0:T(8,128)S(1)}, f32[12,576,576]{1,2,0:T(8,128)}) fusion(f32[12,576,576]{1,2,0:T(8,128)} %get-tuple-element.53, f32[12,576]{1,0:T(8,128)S(1)} %copy-done.29, pred[576,576]{0,1:T(8,128)(4,1)S(1)} %copy-done.11, bf16[576,12,64]{0,2,1:T(8,128)(2,1)} %bitcast.262, bf16[576,12,64]{0,2,1:T(8,128)(2,1)} %bitcast.259), kind=kOutput, calls=%fused_computation.24 | convolution fusion | flops 529507584 | bytes 34007040 | tf_op jit(solution)/shard_map/qhd,khd->hqk/dot_general | solution.py:265
  835.7 13.1 multiply_convert_fusion
  867.5 15.5 scatter_custom_fusion.1
  894.3 39.2 %all-reduce.18 = (f32[768]{0:T(1024)}, f32[768]{0:T(1024)}, f32[768]{0:T(1024)}, f32[768]{0:T(1024)}, f32[768]{0:T(1024)}, /*index=5*/f32[768]{0:T(1024)}, f32[768]{0:T(1024)}) all-reduce(f32[768]{0:T(1024)} %get-tuple-element.20, f32[768]{0:T(1024)} %get-tuple-element.23, ...), channel_id=2, replica_groups=mesh['rep'=4,'exp'=8] {'rep','exp'}, use_global_device_ids=true, to_apply=%region_24.25.clone | all-reduce | flops 5376 | bytes 43008
  954.7 66.8 %reduce-scatter.26.cloned.1.call-done = bf16[4,768,768]{2,1,0:T(8,128)(2,1)} async-done(((bf16[4,3072,768]{2,1,0:T(8,128)(2,1)}), bf16[4,768,768]{2,1,0:T(8,128)(2,1)}) %reduce-scatter.26.cloned.1.call-update) | async-done | bytes 4718608 | tf_op jit(solution)/shard_map/reduce_scatter | solution.py:242
  1028.4 93.5 %reduce-scatter.30.cloned.1.call-done = f32[24,32]{1,0:T(8,128)} async-done(((f32[768,32]{1,0:T(8,128)}), f32[24,32]{1,0:T(8,128)}) %reduce-scatter.30.cloned.1.call-update) | async-done | bytes 3088
  1122.0 100.3 %reduce-scatter.32.cloned.1.call-done = f32[32,24]{0,1:T(8,128)} async-done(((f32[32,768]{0,1:T(8,128)}), f32[32,24]{0,1:T(8,128)}) %reduce-scatter.32.cloned.1.call-update) | async-done | bytes 3088
  1222.2 103.9 %reduce-scatter.22.cloned.1.call-done = f32[24,768]{1,0:T(8,128)} async-done(((f32[768,768]{1,0:T(8,128)}), f32[24,768]{1,0:T(8,128)}) %reduce-scatter.22.cloned.1.call-update) | async-done | bytes 73744 | tf_op jit(solution)/shard_map/reduce_scatter | solution.py:314
  1326.1 104.7 %reduce-scatter.20.cloned.1.call-done = f32[24,768]{1,0:T(8,128)} async-done(((f32[768,768]{1,0:T(8,128)}), f32[24,768]{1,0:T(8,128)}) %reduce-scatter.20.cloned.1.call-update) | async-done | bytes 73744 | tf_op jit(solution)/shard_map/reduce_scatter | solution.py:312
  1430.8 103.9 %reduce-scatter.18.cloned.1.call-done = f32[24,768]{1,0:T(8,128)} async-done(((f32[768,768]{1,0:T(8,128)}), f32[24,768]{1,0:T(8,128)}) %reduce-scatter.18.cloned.1.call-update) | async-done | bytes 73744 | tf_op jit(solution)/shard_map/reduce_scatter | solution.py:311
  1534.6 104.7 %reduce-scatter.16.cloned.1.call-done = f32[24,768]{1,0:T(8,128)} async-done(((f32[768,768]{1,0:T(8,128)}), f32[24,768]{1,0:T(8,128)}) %reduce-scatter.16.cloned.1.call-update) | async-done | bytes 73744 | tf_op jit(solution)/shard_map/reduce_scatter | solution.py:309
  (337 shorter events, 241.4 us)
Async XLA Ops:
  7.2 67.4 %all-gather.7.cloned.1.call-start = ((), (), s32[]{:S(2)}) async-start(), calls=%async_computation.14 | async-start | bytes 1216512 | tf_op jit(solution)/shard_map/all_gather | solution.py:80
  7.9 116.6 %all-gather.5.cloned.1.call-start = ((), (), s32[]{:S(2)}) async-start(), calls=%async_computation.13 | async-start | bytes 1216512 | tf_op jit(solution)/shard_map/all_gather | solution.py:83
  8.7 172.0 %all-gather.9.cloned.1.call-start = ((), (), s32[]{:S(2)}) async-start(), calls=%async_computation.15 | async-start | bytes 1216512 | tf_op jit(solution)/shard_map/all_gather | solution.py:82
  9.4 227.3 %all-gather.11.cloned.1.call-start = ((), (), s32[]{:S(2)}) async-start(), calls=%async_computation.16 | async-start | bytes 1216512 | tf_op jit(solution)/shard_map/all_gather | solution.py:85
  12.9 49.5 %copy-start.66 = (s32[1,576]{1,0:T(1,128)S(1)}, s32[1,576]{1,0:T(1,128)}, u32[]{:S(2)}) copy-start(s32[1,576]{1,0:T(1,128)} %param.23) | copy-start | bytes 6916
  12.9 49.6 %copy-start.4 = (bf16[1,576,768]{2,1,0:T(8,128)(2,1)S(1)}, bf16[1,576,768]{2,1,0:T(8,128)(2,1)}, u32[]{:S(2)}) copy-start(bf16[1,576,768]{2,1,0:T(8,128)(2,1)} %param.22) | copy-start | bytes 2654212
  15.7 57.2 %copy-start.33 = (s32[1152]{0:T(1024)}, s32[1152]{0:T(1024)S(1)}, u32[]{:S(2)}) copy-start(s32[1152]{0:T(1024)S(1)} %mul.267) | copy-start | bytes 13828
  62.3 118.4 %copy-start.41 = (f32[768]{0:T(1024)}, f32[768]{0:T(1024)S(1)}, u32[]{:S(2)}) copy-start(f32[768]{0:T(1024)S(1)} %convert_element_type.191) | copy-start | bytes 9220
  62.3 118.4 %copy-start.64 = (f32[768]{0:T(1024)}, f32[768]{0:T(1024)S(1)}, u32[]{:S(2)}) copy-start(f32[768]{0:T(1024)S(1)} %convert_element_type.192) | copy-start | bytes 9220
  62.3 177.9 %copy-start.43 = (f32[768]{0:T(1024)}, f32[768]{0:T(1024)S(1)}, u32[]{:S(2)}) copy-start(f32[768]{0:T(1024)S(1)} %convert_element_type.204) | copy-start | bytes 9220
  62.7 118.0 %copy-start.35 = (f32[576]{0:T(1024)}, f32[576]{0:T(1024)S(1)}, u32[]{:S(2)}) copy-start(f32[576]{0:T(1024)S(1)} %broadcast_multiply_fusion.1) | copy-start | bytes 6916
  63.2 117.5 %copy-start.51 = (f32[576]{0:T(1024)}, f32[576]{0:T(1024)S(1)}, u32[]{:S(2)}) copy-start(f32[576]{0:T(1024)S(1)} %fusion.88) | copy-start | bytes 6916
  74.5 129.1 %copy-start.10 = (pred[576,576]{0,1:T(8,128)(4,1)}, pred[576,576]{0,1:T(8,128)(4,1)S(1)}, u32[]{:S(2)}) copy-start(pred[576,576]{0,1:T(8,128)(4,1)S(1)} %fusion.72) | copy-start | bytes 995332
  77.6 107.8 %copy-start.12 = (bf16[576,768]{0,1:T(8,128)(2,1)}, bf16[576,768]{0,1:T(8,128)(2,1)S(1)}, u32[]{:S(2)}) copy-start(bf16[576,768]{0,1:T(8,128)(2,1)S(1)} %copy.127) | copy-start | bytes 2654212
  240.6 270.1 %copy-start.14 = (bf16[576,768]{1,0:T(8,128)(2,1)}, bf16[576,768]{1,0:T(8,128)(2,1)S(1)}, u32[]{:S(2)}) copy-start(bf16[576,768]{1,0:T(8,128)(2,1)S(1)} %add_convert_fusion) | copy-start | bytes 2654212
  272.3 48.7 %all-to-all-start = ((bf16[8,4,38,768]{3,1,2,0:T(4,128)(2,1)}), bf16[8,4,38,768]{3,1,2,0:T(4,128)(2,1)}, u32[]{:S(2)}, u32[]{:S(2)}) async-start(bf16[8,4,38,768]{3,1,2,0:T(4,128)(2,1)} %copy.136), calls=%async_computation | async-start | bytes 3735552 | tf_op jit(solution)/shard_map/all_to_all | solution.py:172
  276.9 88.9 %copy-start.47 = (f32[4,3072]{1,0:T(4,128)}, f32[4,3072]{1,0:T(4,128)S(1)}, u32[]{:S(2)}) copy-start(f32[4,3072]{1,0:T(4,128)S(1)} %convert_element_type.208) | copy-start | bytes 147460
  379.2 82.0 %copy-start.16 = (bf16[1,576,768]{2,1,0:T(8,128)(2,1)S(1)}, bf16[1,576,768]{2,1,0:T(8,128)(2,1)}, u32[]{:S(2)}) copy-start(bf16[1,576,768]{2,1,0:T(8,128)(2,1)} %param.43) | copy-start | bytes 2654212
  382.0 129.2 %all-to-all-start.1 = ((bf16[8,4,38,768]{3,1,2,0:T(4,128)(2,1)}), bf16[8,4,38,768]{3,1,2,0:T(4,128)(2,1)}, u32[]{:S(2)}, u32[]{:S(2)}) async-start(bf16[8,4,38,768]{3,1,2,0:T(4,128)(2,1)} %copy.138), calls=%async_computation.1 | async-start | bytes 3735552 | tf_op jit(solution)/shard_map/all_to_all | solution.py:179
  386.3 479.5 %reduce-scatter.28.cloned.1.call-start = ((), (), s32[]{:S(2)}) async-start(), calls=%async_computation.23 | async-start | bytes 983040
  468.3 42.2 %copy-start.67 = (s32[2]{0:T(128)S(1)}, s32[2]{0:T(128)}, u32[]{:S(2)}) copy-start(s32[2]{0:T(128)} %constant.142) | copy-start | bytes 28
  577.4 47.6 %copy-start.48 = (f32[4,3072]{1,0:T(4,128)S(1)}, f32[4,3072]{1,0:T(4,128)}, u32[]{:S(2)}) copy-start(f32[4,3072]{1,0:T(4,128)} %copy-done.47) | copy-start | bytes 147460
  647.8 299.8 %reduce-scatter.24.cloned.1.call-start = ((), (), s32[]{:S(2)}) async-start(), calls=%async_computation.21 | async-start | bytes 23592960 | tf_op jit(solution)/shard_map/reduce_scatter | solution.py:236
  664.9 356.6 %reduce-scatter.26.cloned.1.call-start = ((), (), s32[]{:S(2)}) async-start(), calls=%async_computation.22 | async-start | bytes 23592960 | tf_op jit(solution)/shard_map/reduce_scatter | solution.py:242
  700.3 48.5 %all-to-all-start.3 = ((bf16[8,4,38,768]{3,1,2,0:T(4,128)(2,1)}), bf16[8,4,38,768]{3,1,2,0:T(4,128)(2,1)}, u32[]{:S(2)}, u32[]{:S(2)}) async-start(bf16[8,4,38,768]{3,1,2,0:T(4,128)(2,1)} %copy.144), calls=%async_computation.3 | async-start | bytes 3735552 | tf_op jit(solution)/shard_map/all_to_all | solution.py:220
  704.6 417.4 %reduce-scatter.30.cloned.1.call-start = ((), (), s32[]{:S(2)}) async-start(), calls=%async_computation.24 | async-start | bytes 405504
  705.9 516.3 %reduce-scatter.32.cloned.1.call-start = ((), (), s32[]{:S(2)}) async-start(), calls=%async_computation.25 | async-start | bytes 405504
  718.6 607.4 %reduce-scatter.22.cloned.1.call-start = ((), (), s32[]{:S(2)}) async-start(), calls=%async_computation.20 | async-start | bytes 2433024 | tf_op jit(solution)/shard_map/reduce_scatter | solution.py:314
  795.5 635.3 %reduce-scatter.20.cloned.1.call-start = ((), (), s32[]{:S(2)}) async-start(), calls=%async_computation.19 | async-start | bytes 2433024 | tf_op jit(solution)/shard_map/reduce_scatter | solution.py:312
  835.4 699.2 %reduce-scatter.18.cloned.1.call-start = ((), (), s32[]{:S(2)}) async-start(), calls=%async_computation.18 | async-start | bytes 2433024 | tf_op jit(solution)/shard_map/reduce_scatter | solution.py:311
  856.2 783.1 %reduce-scatter.16.cloned.1.call-start = ((), (), s32[]{:S(2)}) async-start(), calls=%async_computation.17 | async-start | bytes 2433024 | tf_op jit(solution)/shard_map/reduce_scatter | solution.py:309
  891.6 52.5 %copy-start.18 = (bf16[1,576,768]{2,1,0:T(8,128)(2,1)S(1)}, bf16[1,576,768]{2,1,0:T(8,128)(2,1)}, u32[]{:S(2)}) copy-start(bf16[1,576,768]{2,1,0:T(8,128)(2,1)} %param.43) | copy-start | bytes 2654212
  (63 other events, 659.4 us)
Sparse Core Ops, SparseCore 0:
  11.1 57.0 all-gather.6
  71.1 53.3 all-gather.4
  127.5 53.1 all-gather.8
  183.6 53.1 all-gather.10
  647.9 24.0 reduce-scatter.27
  675.0 170.7 reduce-scatter.23
  849.2 172.2 reduce-scatter.25
  1027.1 94.8 reduce-scatter.29
  1128.3 93.9 reduce-scatter.31
  1227.9 98.1 reduce-scatter.21
  1332.8 97.9 reduce-scatter.19
  1436.5 98.1 reduce-scatter.17
  1541.4 97.9 reduce-scatter.15
where the time goes:
time: 1660 us; the launch traced here: 1650 us
  waiting for transfers between devices  876 us (53%)
  blocking collectives  240 us (14%)
  matrix products  220 us (13%)
  other arithmetic  169 us (10%)
  local copies, waits for them, and re-layouts  111 us (7%)
    unnamed x16, waiting for transfers between devices  197 us
    reduce_scatter x1, waiting for transfers between devices, body(): lax.psum_scatter(query_w_grad, ('rep', 'exp'), scatter_dimension=0, tiled...  105 us
    reduce_scatter x1, waiting for transfers between devices, body(): lax.psum_scatter(value_w_grad, ('rep', 'exp'), scatter_dimension=0, tiled...  105 us
    reduce_scatter x1, waiting for transfers between devices, body(): lax.psum_scatter(key_w_grad, ('rep', 'exp'), scatter_dimension=0, tiled=T...  104 us
    reduce_scatter x1, waiting for transfers between devices, body(): lax.psum_scatter(proj_w_grad, ('rep', 'exp'), scatter_dimension=0, tiled=...  104 us
    unnamed x2, blocking collectives  81.9 us
    all_gather x1, blocking collectives, body(): lax.all_gather(expert_out_bias, ('rep', 'exp'), axis=1, tiled=True)  74.1 us
    reduce_scatter x1, waiting for transfers between devices, body(): lax.psum_scatter(out_w_grad.astype(jnp.bfloat16), 'rep', scatter_dimensio...  66.8 us
  transfers between devices with their start and end apart: 16, of which 12 were waited for; matrix products, arithmetic and copies ran while one was open for 19% of the time, Pallas kernels for 0%

commit v1 on v0

--- a/solution.py
+++ b/solution.py
@@ -1,10 +1,258 @@
+import functools
 import jax
 import jax.numpy as jnp
 from jax import lax
+from jax.experimental import pallas as pl
+from jax.experimental.pallas import tpu as pltpu
 from jax.sharding import PartitionSpec as P
 
 HEADS = 12
 EXPERTS = 32
+MESH = pl.DeviceIdType.MESH
+MIB = 1 << 20
+
+def bit_dims(reps, groups):
+    rb, gb = reps.bit_length() - 1, groups.bit_length() - 1
+    return [(0, 1 << k) for k in reversed(range(rb))] + [(1, 1 << k) for k in reversed(range(gb))]
+
+def orders(dims):
+    last = len(dims) - 1
+    rep = [i for i, d in enumerate(dims) if d[0] == 0]
+    exp = [i for i, d in enumerate(dims) if d[0] == 1 and i != last]
+    exp = exp[::-1]
+    return [[last] + rep + exp, [last] + rep[::-1] + exp, [last] + exp + rep]
+
+def my_bits(dims):
+    at = (lax.axis_index("rep"), lax.axis_index("exp"))
+    return [(at[a] // s) % 2 for a, s in dims], at
+
+def partner(dims, at, i):
+    a, s = dims[i]
+    bit = (at[a] // s) % 2
+    there = at[a] + (1 - 2 * bit) * s
+    return (there, at[1]) if a == 0 else (at[0], there)
+
+def greet(dims, at):
+    barrier = pltpu.get_barrier_semaphore()
+    for i in range(len(dims)):
+        pl.semaphore_signal(barrier, inc=1, device_id=partner(dims, at, i), device_id_type=MESH)
+    pl.semaphore_wait(barrier, len(dims))
+
+def gather_kernel(dims, widths, count, *refs):
+    ins, small_in = refs[:count], refs[count]
+    outs, small_out = refs[count + 1:2 * count + 1], refs[2 * count + 1]
+    own_sem, send_sem, recv_sem = refs[2 * count + 2:]
+    bits, at = my_bits(dims)
+    n = len(dims)
+    own = [pltpu.make_async_copy(a, o.at[tuple(bits)], own_sem.at[i]) for i, (a, o) in enumerate(zip(ins + (small_in,), outs + (small_out,)))]
+    for c in own: c.start()
+    greet(dims, at)
+    for c in own: c.wait()
+    plan = [o[::-1] for o in orders(dims)]
+    parts = len(plan)
+    def copies(p, k):
+        done = plan[p][:k]
+        i = plan[p][k]
+        lead = tuple(slice(None) if j in done else bits[j] for j in range(n))
+        out = []
+        for a, o in enumerate(outs):
+            where = o.at[lead + (slice(None), pl.ds(widths[p][0], widths[p][1]))]
+            out.append(pltpu.make_async_remote_copy(where, where, send_sem.at[p, k, a], recv_sem.at[p, k, a], device_id=partner(dims, at, i), device_id_type=MESH))
+        if p == 0:
+            where = small_out.at[lead]
+            out.append(pltpu.make_async_remote_copy(where, where, send_sem.at[p, k, count], recv_sem.at[p, k, count], device_id=partner(dims, at, i), device_id_type=MESH))
+        return out
+    live = []
+    for k in range(n):
+        for p in range(parts):
+            if k > 0:
+                for c in live[(k - 1) * parts + p]: c.wait_recv()
+            cs = copies(p, k)
+            for c in cs: c.start()
+            live.append(cs)
+    for p in range(parts):
+        for c in live[(n - 1) * parts + p]: c.wait_recv()
+    for cs in live:
+        for c in cs: c.wait_send()
+
+def gather_params(weights, small, reps, groups, space=pl.ANY):
+    dims = bit_dims(reps, groups)
+    n = len(dims)
+    rows, cols = weights[0].shape
+    third = cols // 3 // 128 * 128
+    widths = [(0, third), (third, third), (2 * third, cols - 2 * third)]
+    count = len(weights)
+    lead = (2,) * n
+    outs = pl.pallas_call(
+        functools.partial(gather_kernel, dims, widths, count),
+        out_shape=[jax.ShapeDtypeStruct(lead + w.shape, w.dtype) for w in weights] + [jax.ShapeDtypeStruct(lead + small.shape, small.dtype)],
+        in_specs=[pl.BlockSpec(memory_space=space)] * (count + 1),
+        out_specs=[pl.BlockSpec(memory_space=space)] * (count + 1),
+        scratch_shapes=[pltpu.SemaphoreType.DMA((count + 1,)), pltpu.SemaphoreType.DMA((3, n, count + 1)), pltpu.SemaphoreType.DMA((3, n, count + 1))],
+        compiler_params=pltpu.CompilerParams(collective_id=0, has_side_effects=True, vmem_limit_bytes=40 * MIB),
+    )(*weights, small)
+    return [o.reshape((reps * groups * o.shape[-2], o.shape[-1])) for o in outs[:count]], outs[count].reshape((reps * groups,) + small.shape)
+
+def scatter_kernel(dims, widths, count, *refs):
+    ins, small_in = refs[:count], refs[count]
+    outs, small_out = refs[count + 1:2 * count + 1], refs[2 * count + 1]
+    n = len(dims)
+    scr = refs[2 * count + 2:]
+    parts = 3
+    send_sem, recv_sem = scr[:2]
+    scr = scr[2:]
+    take = iter(scr)
+    bufs = [[(next(take), next(take), next(take) if k < n - 1 else None) for p in range(parts)] for k in range(n)]
+    smalls = [(next(take), next(take) if k < n - 1 else None) for k in range(n)]
+    bits, at = my_bits(dims)
+    plan = orders(dims)
+    left = [list(range(n)) for _ in range(parts)]
+    small_left = list(range(n))
+    small_cur = small_in
+    def split(have, i, b):
+        return tuple(b if j == i else slice(None) for j in have)
+    live = []
+    def begin(k, p):
+        i = plan[p][k]
+        sb, rb, _ = bufs[k][p]
+        far = split(left[p], i, 1 - bits[i])
+        cols = pl.ds(widths[p][0], widths[p][1]) if k == 0 else slice(None)
+        for a in range(count):
+            src = ins[a][far + (slice(None), cols)] if k == 0 else bufs[k - 1][p][2][(a,) + far]
+            sb[a] = src.astype(sb.dtype)
+        c = [pltpu.make_async_remote_copy(sb, rb, send_sem.at[k, p], recv_sem.at[k, p], device_id=partner(dims, at, i), device_id_type=MESH)]
+        if p == 0:
+            src = (small_in if k == 0 else smalls[k - 1][1]).at[far]
+            c.append(pltpu.make_async_remote_copy(src, smalls[k][0], send_sem.at[k, parts], recv_sem.at[k, parts], device_id=partner(dims, at, i), device_id_type=MESH))
+        for x in c: x.start()
+        return c
+    def finish(k, p, c):
+        i = plan[p][k]
+        sb, rb, acc = bufs[k][p]
+        near = split(left[p], i, bits[i])
+        cols = pl.ds(widths[p][0], widths[p][1]) if k == 0 else slice(None)
+        for x in c: x.wait_recv()
+        for a in range(count):
+            src = ins[a][near + (slice(None), cols)] if k == 0 else bufs[k - 1][p][2][(a,) + near]
+            tot = src + rb[a].astype(jnp.float32)
+            if k < n - 1:
+                acc[a] = tot
+            else:
+                outs[a][:, widths[p][0]:widths[p][0] + widths[p][1]] = tot
+        if p == 0:
+            src = (small_in if k == 0 else smalls[k - 1][1])[near]
+            tot = src + smalls[k][0][...]
+            if k < n - 1:
+                smalls[k][1][...] = tot
+            else:
+                small_out[...] = tot
+        left[p].remove(i)
+    greet(dims, at)
+    live = [begin(0, p) for p in range(parts)]
+    every = list(live)
+    for k in range(n):
+        for p in range(parts):
+            finish(k, p, live[p])
+            if k < n - 1:
+                live[p] = begin(k + 1, p)
+                every.append(live[p])
+    for cs in every:
+        for c in cs: c.wait_send()
+
+def scatter_grads(grads, small, reps, groups, link=jnp.bfloat16):
+    dims = bit_dims(reps, groups)
+    n = len(dims)
+    full, cols = grads[0].shape
+    rows = full // (reps * groups)
+    third = cols // 3 // 128 * 128
+    widths = [(0, third), (third, third), (2 * third, cols - 2 * third)]
+    count = len(grads)
+    lead = (2,) * n
+    grads = [g.reshape(lead + (rows, cols)) for g in grads]
+    small = small.reshape(lead + small.shape[1:])
+    scratch = [pltpu.SemaphoreType.DMA((n, 4)), pltpu.SemaphoreType.DMA((n, 4))]
+    for k in range(n):
+        for p in range(3):
+            shape = (count,) + (2,) * (n - 1 - k) + (rows, widths[p][1])
+            scratch += [pltpu.VMEM(shape, link), pltpu.VMEM(shape, link)]
+            if k < n - 1:
+                scratch.append(pltpu.VMEM(shape, jnp.float32))
+    for k in range(n):
+        shape = (2,) * (n - 1 - k) + small.shape[n:]
+        scratch.append(pltpu.VMEM(shape, jnp.float32))
+        if k < n - 1:
+            scratch.append(pltpu.VMEM(shape, jnp.float32))
+    vm = pl.BlockSpec(memory_space=pltpu.VMEM)
+    outs = pl.pallas_call(
+        functools.partial(scatter_kernel, dims, widths, count),
+        out_shape=[jax.ShapeDtypeStruct((rows, cols), jnp.float32)] * count + [jax.ShapeDtypeStruct(small.shape[n:], jnp.float32)],
+        in_specs=[vm] * (count + 1),
+        out_specs=[vm] * (count + 1),
+        scratch_shapes=scratch,
+        compiler_params=pltpu.CompilerParams(collective_id=1, has_side_effects=True, vmem_limit_bytes=56 * MIB),
+    )(*grads, small)
+    return outs[:count], outs[count]
+
+
+def pack_small(parts, lead):
+    flat = jnp.concatenate([p.reshape(lead + (-1,)) for p in parts], axis=-1)
+    size = flat.shape[-1]
+    room = -(-size // 2048) * 2048
+    flat = jnp.pad(flat, [(0, 0)] * len(lead) + [(0, room - size)])
+    return flat.reshape(lead + (room // 128, 128))
+
+
+def gather_all(vectors, weights, router, shift):
+    axes = ("rep", "exp")
+    reps, groups = lax.axis_size("rep"), lax.axis_size("exp")
+    devices = reps * groups
+    per = weights[0].shape[0]
+    if per % 8 or devices & (devices - 1):
+        return (
+            [lax.all_gather(v, axes, axis=0, tiled=True) for v in vectors],
+            [lax.all_gather(w, axes, axis=0, tiled=True) for w in weights],
+            lax.all_gather(router, axes, axis=0, tiled=True),
+            lax.all_gather(shift, axes, axis=1, tiled=True),
+        )
+    small = pack_small(vectors + [router, shift], ())
+    weights, small = gather_params(weights, small, reps, groups)
+    small = small.reshape(devices, -1)
+    count = len(vectors)
+    got = [small[:, i * per : (i + 1) * per].reshape(-1) for i in range(count)]
+    at = count * per
+    wide = router.shape[1]
+    routers = small[:, at : at + per * wide].reshape(-1, wide)
+    at += per * wide
+    rows = shift.shape[0]
+    shifts = small[:, at : at + rows * per].reshape(devices, rows, per)
+    shifts = jnp.transpose(shifts, (1, 0, 2)).reshape(rows, -1)
+    return got, weights, routers, shifts
+
+
+def scatter_all(vectors, weights, router, shift):
+    axes = ("rep", "exp")
+    reps, groups = lax.axis_size("rep"), lax.axis_size("exp")
+    devices = reps * groups
+    per = weights[0].shape[0] // devices
+    if per % 8 or devices & (devices - 1):
+        return (
+            [lax.psum_scatter(v, axes, scatter_dimension=0, tiled=True) for v in vectors],
+            [lax.psum_scatter(w, axes, scatter_dimension=0, tiled=True) for w in weights],
+            lax.psum_scatter(router, axes, scatter_dimension=0, tiled=True),
+            lax.psum_scatter(shift, axes, scatter_dimension=1, tiled=True),
+        )
+    rows = shift.shape[0]
+    parted = jnp.transpose(shift.reshape(rows, devices, per), (1, 0, 2))
+    small = pack_small(vectors + [router, parted], (devices,))
+    weights, small = scatter_grads(weights, small, reps, groups)
+    small = small.reshape(-1)
+    count = len(vectors)
+    got = [small[i * per : (i + 1) * per] for i in range(count)]
+    at = count * per
+    wide = router.shape[1]
+    routers = small[at : at + per * wide].reshape(per, wide)
+    at += per * wide
+    return got, weights, routers, small[at : at + rows * per].reshape(rows, per)
 
 
 epsilon = 1e-06
@@ -74,36 +322,14 @@
     expert_out_bias,
     cotangent,
 ):
-    gathered = (
-        lax.all_gather(ln1_gain, ("rep", "exp"), axis=0, tiled=True),
-        lax.all_gather(ln1_bias, ("rep", "exp"), axis=0, tiled=True),
-        lax.all_gather(w_query, ("rep", "exp"), axis=0, tiled=True),
-        lax.all_gather(query_bias, ("rep", "exp"), axis=0, tiled=True),
-        lax.all_gather(w_key, ("rep", "exp"), axis=0, tiled=True),
-        lax.all_gather(w_value, ("rep", "exp"), axis=0, tiled=True),
-        lax.all_gather(value_bias, ("rep", "exp"), axis=0, tiled=True),
-        lax.all_gather(w_attn_out, ("rep", "exp"), axis=0, tiled=True),
-        lax.all_gather(attn_out_bias, ("rep", "exp"), axis=0, tiled=True),
-        lax.all_gather(ln2_gain, ("rep", "exp"), axis=0, tiled=True),
-        lax.all_gather(ln2_bias, ("rep", "exp"), axis=0, tiled=True),
-        lax.all_gather(w_router, ("rep", "exp"), axis=0, tiled=True),
-        lax.all_gather(expert_out_bias, ("rep", "exp"), axis=1, tiled=True),
-    )
-    (
-        gain_one,
-        bias_one,
-        query_weight,
-        query_shift,
-        key_weight,
-        value_weight,
-        value_shift,
-        proj_weight,
-        proj_shift,
-        gain_two,
-        bias_two,
-        router_weight,
-        result_shift,
-    ) = gathered
+    vectors, weights, router_weight, result_shift = gather_all(
+        [ln1_gain, ln1_bias, query_bias, value_bias, attn_out_bias, ln2_gain, ln2_bias],
+        [w_query, w_key, w_value, w_attn_out],
+        w_router,
+        expert_out_bias,
+    )
+    gain_one, bias_one, query_shift, value_shift, proj_shift, gain_two, bias_two = vectors
+    query_weight, key_weight, value_weight, proj_weight = weights
     gain_one = gain_one.astype(jnp.float32)
     bias_one = bias_one.astype(jnp.float32)
     gain_two = gain_two.astype(jnp.float32)
@@ -303,40 +529,39 @@
     norm_one_back = jax.vjp(layer_norm, inputs, gain_one, bias_one)[1]
     input_ln_grad, gain_one_grad, bias_one_grad = norm_one_back(normed_grad)
     tokens_grad = residual_grad + input_ln_grad
-    dense_sums = (
-        lax.psum_scatter(gain_one_grad, ("rep", "exp"), scatter_dimension=0, tiled=True),
-        lax.psum_scatter(bias_one_grad, ("rep", "exp"), scatter_dimension=0, tiled=True),
-        lax.psum_scatter(query_w_grad, ("rep", "exp"), scatter_dimension=0, tiled=True),
-        lax.psum_scatter(query_b_grad, ("rep", "exp"), scatter_dimension=0, tiled=True),
-        lax.psum_scatter(key_w_grad, ("rep", "exp"), scatter_dimension=0, tiled=True),
-        lax.psum_scatter(value_w_grad, ("rep", "exp"), scatter_dimension=0, tiled=True),
-        lax.psum_scatter(value_b_grad, ("rep", "exp"), scatter_dimension=0, tiled=True),
-        lax.psum_scatter(proj_w_grad, ("rep", "exp"), scatter_dimension=0, tiled=True),
-        lax.psum_scatter(proj_b_grad, ("rep", "exp"), scatter_dimension=0, tiled=True),
-        lax.psum_scatter(gain_two_grad, ("rep", "exp"), scatter_dimension=0, tiled=True),
-        lax.psum_scatter(bias_two_grad, ("rep", "exp"), scatter_dimension=0, tiled=True),
-        lax.psum_scatter(router_w_grad, ("rep", "exp"), scatter_dimension=0, tiled=True),
-        lax.psum_scatter(shift_grad, ("rep", "exp"), scatter_dimension=1, tiled=True),
+    vector_sums, weight_sums, router_sum, shift_sum = scatter_all(
+        [
+            gain_one_grad,
+            bias_one_grad,
+            query_b_grad,
+            value_b_grad,
+            proj_b_grad,
+            gain_two_grad,
+            bias_two_grad,
+        ],
+        [query_w_grad, key_w_grad, value_w_grad, proj_w_grad],
+        router_w_grad,
+        shift_grad,
     )
     return (
         output.astype(jnp.bfloat16)[None],
         tokens_grad[None],
-        dense_sums[0],
-        dense_sums[1],
-        dense_sums[2],
-        dense_sums[3],
-        dense_sums[4],
-        dense_sums[5],
-        dense_sums[6],
-        dense_sums[7],
-        dense_sums[8],
-        dense_sums[9],
-        dense_sums[10],
-        dense_sums[11],
+        vector_sums[0],
+        vector_sums[1],
+        weight_sums[0],
+        vector_sums[2],
+        weight_sums[1],
+        weight_sums[2],
+        vector_sums[3],
+        weight_sums[3],
+        vector_sums[4],
+        vector_sums[5],
+        vector_sums[6],
+        router_sum,
         expert_sums[0],
         expert_sums[1],
         expert_sums[2],
-        dense_sums[12],
+        shift_sum,
     )
 
 

time: 1660 us -> 852 us (0.51)
  waiting for transfers between devices: 876 us -> 178 us
  blocking collectives: 240 us -> 46.6 us
  Pallas kernels: 0 us -> 92.2 us
    reduce_scatter x4 -> x0, waiting for transfers between devices: 417 us -> none  [the longest x1 105 us: body(): lax.psum_scatter(query_w_grad, ('rep', 'exp'), scatter_dimension=0, tiled...]
    unnamed x16 -> x4, waiting for transfers between devices: 197 us -> 0.05 us
    all_gather x4 -> x0, waiting for transfers between devices: 121 us -> none  [the longest x1 52.5 us: body(): lax.all_gather(w_key, ('rep', 'exp'), axis=0, tiled=True)]
    all_gather x2 -> x0, blocking collectives: 111 us -> none  [the longest x1 74.1 us: body(): lax.all_gather(expert_out_bias, ('rep', 'exp'), axis=1, tiled=True)]
    pallas_call x0 -> x2, Pallas kernels: none -> 92.2 us  [the longest x1 54.3 us: scatter_grads(): pl.pallas_call(functools.partial(scatter_kernel, dims, widths, count), ou...]
    unnamed x2 -> x0, blocking collectives: 81.9 us -> none
    all_to_all x1, waiting for transfers between devices: 0.01 us -> 30.1 us  [body(): lax.all_to_all(result.astype(jnp.bfloat16), 'exp', split_axis=0, concat_a...]
  transfers between devices with their start and end apart: 16 -> 6, of which waited for: 12 -> 4; matrix products, arithmetic and copies ran while one was open for 19% -> 28% of each run, Pallas kernels for 0% -> 6%
where the time goes in v1:
time: 852 us; the launch traced here: 845 us
  matrix products  213 us (25%)
  waiting for transfers between devices  178 us (21%)
  other arithmetic  174 us (20%)
  local copies, waits for them, and re-layouts  112 us (13%)
  Pallas kernels  92.2 us (11%)
  blocking collectives  46.6 us (5%)
  between operations  15.8 us (2%)
  starting transfers between devices  13.7 us (2%)
    reduce_scatter x1, waiting for transfers between devices, body(): lax.psum_scatter(out_w_grad.astype(jnp.bfloat16), 'rep', scatter_dimensio...  76.4 us
    pallas_call x1, Pallas kernels, scatter_grads(): pl.pallas_call(functools.partial(scatter_kernel, dims, widths, count), ou...  54.3 us
    all_to_all x1, blocking collectives, body(): lax.all_to_all(slot_grad, 'exp', split_axis=0, concat_axis=0, tiled=True)  46.6 us
    all_to_all x1, waiting for transfers between devices, body(): lax.all_to_all(outgoing, 'exp', split_axis=0, concat_axis=0, tiled=True)  44.1 us
    dot_general x1, matrix products, body(): jnp.einsum('secd,edf->secf', received, expert_in, preferred_element_type=...  43.5 us
    pallas_call x1, Pallas kernels, gather_params(): pl.pallas_call(functools.partial(gather_kernel, dims, widths, count), out...  37.9 us
    scatter-add x1, other arithmetic, body(): jnp.zeros((length, feature_dim), jnp.float32).at[seq_token]  30.4 us
    all_to_all x1, waiting for transfers between devices, body(): lax.all_to_all(result.astype(jnp.bfloat16), 'exp', split_axis=0, concat_a...  30.1 us
  transfers between devices with their start and end apart: 6, of which 4 were waited for; matrix products, arithmetic and copies ran while one was open for 28% of the time, Pallas kernels for 6%

profile of v1, /device:TPU:0, one launch (start us, length us, event | category | flops | bytes accessed | tf_op | source)
XLA Modules:
  0.0 845.1 jit_solution(2795413372916998488)
XLA Ops:
  18.3 9.1 %reduce-window.6 = s32[32,9,128]{2,1,0:T(8,128)S(1)} reduce-window(s32[32,9,128]{2,1,0:T(8,128)S(1)} %fusion.79, s32[]{:T(128)} %constant.48.clone.1), window={size=1x1x128 pad=0_0x0_0x127_0}, to_apply=%region_8.9 | reduce-window | flops 4681728 | bytes 294916 | tf_op jit(solution)/shard_map/reduce-window
  28.6 37.9 %shard_map.349 = (bf16[2,2,2,2,2,24,768]{6,5,4,3,2,1,0:T(8,128)(2,1)S(1)}, bf16[2,2,2,2,2,24,768]{6,5,4,3,2,1,0:T(8,128)(2,1)S(1)}, bf16[2,2,2,2,2,24,768]{6,5,4...) custom-call(bf16[24,768]{1,0:T(8,128)(2,1)S(1)} %copy-done.2, ...), custom_call_target="tpu_custom_call" | custom-call | tf_op jit(solution)/shard_map/pallas_call | solution.py:86
  83.2 10.4 %fusion.30 = (f32[12,576]{1,0:T(8,128)S(1)}, f32[12,576,576]{1,2,0:T(8,128)}) fusion(pred[576,576]{0,1:T(8,128)(4,1)S(1)} %fusion.72, bf16[576,12,64]{0,2,1:T(8,128)(2,1)} %bitcast.303, bf16[576,12,64]{0,2,1:T(8,128)(2,1)S(1)} %bitcast.301), kind=kOutput, calls=%fused_computation.58 | convolution fusion | flops 521544960 | bytes 18054144 | tf_op jit(solution)/shard_map/qhd,khd->hqk/dot_general | solution.py:285
  93.6 9.8 %exponential_reduce_fusion = f32[12,576]{1,0:T(8,128)S(1)} fusion(f32[12,576,576]{1,2,0:T(8,128)} %get-tuple-element.133, f32[12,576]{1,0:T(8,128)S(1)} %get-tuple-element.132, pred[576,576]{0,1:T(8,128)(4,1)S(1)} %fusion.72), kind=kLoop, calls=%fused_computation.26 | loop fusion | flops 15918336 | bytes 16312320 | tf_op jit(solution)/shard_map/reduce_sum | solution.py:292
  103.4 10.6 %convolution_convert_fusion.1 = bf16[12,64,576]{2,1,0:T(8,128)(2,1)S(1)} fusion(bf16[576,12,64]{0,2,1:T(8,128)(2,1)S(1)} %bitcast.305, f32[12,576,576]{1,2,0:T(8,128)} %get-tuple-element.133, f32[12,576]{1,0:T(8,128)S(1)} %log_add_fusion, pred[576,576]{0,1:T(8,128)(4,1)S(1)} %fusion.72), kind=kOutput, calls=%fused_computation.121 | convolution fusion | flops 525975552 | bytes 18054144 | tf_op jit(solution)/shard_map/hqk,khd->qhd/dot_general | solution.py:369
  119.0 20.7 %scatter_custom_fusion = bf16[1217,768]{1,0:T(8,128)(2,1)S(1)} fusion(s32[1152]{0:T(1024)S(1)} %get-tuple-element.101, bf16[576,768]{1,0:T(8,128)(2,1)S(1)} %add_convert_fusion, s32[2048]{0:T(1024)S(1)} %get-tuple-element.149, bf16[]{:T(256)} %constant.47.clone.1), kind=kCustom, calls=%fused_computation.103 | custom fusion | flops 884736 | bytes 1869314 | tf_op jit(solution)/shard_map/scatter-add | solution.py:392
  150.1 44.1 %all-to-all-done = bf16[8,4,38,768]{3,1,2,0:T(4,128)(2,1)S(1)} async-done(((bf16[8,4,38,768]{3,1,2,0:T(4,128)(2,1)}), bf16[8,4,38,768]{3,1,2,0:T(4,128)(2,1)S(1)}, u32[]{:S(2)}, u32[]{:S(2)}) %all-to-all-start) | async-done | bytes 1867808 | tf_op jit(solution)/shard_map/all_to_all | solution.py:398
  194.2 43.5 %fusion.17 = (bf16[8,4,38,3072]{3,2,0,1:T(8,128)(2,1)S(1)}, f32[8,4,38,3072]{3,2,0,1:T(8,128)}, f32[4,8,38,3072]{3,2,1,0:T(8,128)}) fusion(f32[4,3072]{1,0:T(4,128)S(1)} %convert_element_type.284, bf16[4,768,3072]{2,1,0:T(8,128)(2,1)} %param.39, bf16[8,4,38,768]{3,1,2,0:T(4,128)(2,1)S(1)} %all-to-all-done), kind=kOutput, calls=%fused_computation.44 | convolution fusion | flops 5984354304 | bytes 58146816 | tf_op jit(solution)/shard_map/secd,edf->secf/dot_general | solution.py:400
  237.7 13.3 %convert_bitcast_fusion.2 = bf16[8,4,38,768]{3,2,0,1:T(8,128)(2,1)S(1)} fusion(bf16[8,4,38,3072]{3,2,0,1:T(8,128)(2,1)S(1)} %get-tuple-element.108, bf16[4,3072,768]{2,1,0:T(8,128)(2,1)} %param.41), kind=kOutput, calls=%fused_computation.85 | convolution fusion | flops 5738741760 | bytes 28213248 | tf_op jit(solution)/shard_map/secf,efd->secd/dot_general | solution.py:404
  258.3 5.1 gather_fusion.4
  272.1 30.1 %all-to-all-done.1 = bf16[8,4,38,768]{3,1,2,0:T(4,128)(2,1)} async-done(((bf16[8,4,38,768]{3,1,2,0:T(4,128)(2,1)}), bf16[8,4,38,768]{3,1,2,0:T(4,128)(2,1)}, u32[]{:S(2)}, u32[]{:S(2)}) %all-to-all-start.1) | async-done | bytes 1867808 | tf_op jit(solution)/shard_map/all_to_all | solution.py:405
  317.7 7.8 gather_fusion.3
  329.0 7.3 scatter_custom_fusion.4
  336.4 9.7 %gather_fusion.1 = f32[1152]{0:T(1024)S(1)} fusion(f32[576,32]{0,1:T(8,128)S(1)} %get-tuple-element.107, s32[1152]{0:T(1024)S(1)} %copy-done.17), kind=kCustom, calls=%fused_computation.1 | custom fusion | bytes 18432 | tf_op jit(solution)/shard_map/gather | solution.py:417
  346.2 16.6 %scatter_custom_fusion.2 = f32[1217,768]{1,0:T(8,128)} fusion(s32[1152]{0:T(1024)} %copy-done.84, f32[1152,768]{1,0:T(8,128)} %gather_fusion.4, f32[]{:T(128)} %constant.44.clone.1, f32[1152]{0:T(1024)S(1)} %convert_multiply_fusion.1), kind=kCustom, calls=%fused_computation.62 | custom fusion | flops 1769472 | bytes 7282688 | tf_op jit(solution)/shard_map/scatter-add | solution.py:430
  369.5 46.6 %all_to_all.20 = bf16[8,4,38,768]{3,1,2,0:T(4,128)(2,1)S(1)} all-to-all(bf16[8,4,38,768]{3,1,2,0:T(4,128)(2,1)S(1)} %copy.136), channel_id=1, replica_groups=mesh['rep'=4,'exp'=8] {'exp'}, dimensions={0} | all-to-all | bytes 3735552 | tf_op jit(solution)/shard_map/all_to_all | solution.py:437
  416.0 22.4 %fusion.113 = (bf16[4,3072]{1,0:T(4,128)(2,1)S(1)}, bf16[8,4,38,3072]{3,2,0,1:T(8,128)(2,1)}) fusion(f32[8,4,38,3072]{3,2,0,1:T(8,128)} %get-tuple-element.109, bf16[4,3072,768]{2,1,0:T(8,128)(2,1)} %param.41, bf16[8,4,38,768]{3,1,2,0:T(4,128)(2,1)S(1)} %all_to_all.20, f32[4,8,38,3072]{3,2,1,0:T(8,128)} %get-tuple-element.136, f32[4,3072]{1,0:T(4,128)S(1)} %copy-done.71), kind=kOutput, calls=%fused_computation.205 | convolution fusion | flops 5797564416 | bytes 58171392 | tf_op jit(solution)/shard_map/secd,efd->secf/dot_general | solution.py:438
  439.7 16.7 %bitcast_convert_fusion.1 = bf16[4,768,3072]{2,1,0:T(8,128)(2,1)} fusion(bf16[8,4,38,3072]{3,2,0,1:T(8,128)(2,1)} %get-tuple-element.147, bf16[8,4,38,768]{3,1,2,0:T(4,128)(2,1)S(1)} %copy-done.35), kind=kOutput, calls=%fused_computation.13 | convolution fusion | flops 5747245056 | bytes 28213248 | tf_op jit(solution)/shard_map/secd,secf->edf/dot_general | solution.py:459
  457.9 19.6 %bitcast_convert_fusion = bf16[4,3072,768]{2,1,0:T(8,128)(2,1)} fusion(bf16[8,4,38,3072]{3,2,0,1:T(8,128)(2,1)} %copy-done.105, bf16[8,4,38,768]{3,1,2,0:T(4,128)(2,1)S(1)} %copy-done.37), kind=kOutput, calls=%fused_computation.12 | convolution fusion | flops 5747245056 | bytes 28213248 | tf_op jit(solution)/shard_map/secf,secd->efd/dot_general | solution.py:458
  477.5 12.8 %convert_bitcast_fusion.1 = bf16[8,4,38,768]{3,2,0,1:T(8,128)(2,1)S(1)} fusion(bf16[8,4,38,3072]{3,2,0,1:T(8,128)(2,1)} %get-tuple-element.147, bf16[4,768,3072]{2,1,0:T(8,128)(2,1)} %param.39), kind=kOutput, calls=%fused_computation.84 | convolution fusion | flops 5738741760 | bytes 28213248 | tf_op jit(solution)/shard_map/secf,edf->secd/dot_general | solution.py:443
  493.0 4.7 all-to-all-start.3
  514.2 27.6 %all-to-all-done.3 = bf16[8,4,38,768]{3,1,2,0:T(4,128)(2,1)} async-done(((bf16[8,4,38,768]{3,1,2,0:T(4,128)(2,1)}), bf16[8,4,38,768]{3,1,2,0:T(4,128)(2,1)}, u32[]{:S(2)}, u32[]{:S(2)}) %all-to-all-start.3) | async-done | bytes 1867808 | tf_op jit(solution)/shard_map/all_to_all | solution.py:446
  549.0 30.4 %scatter_custom_fusion.3 = f32[576,768]{1,0:T(8,128)} fusion(f32[576,768]{1,0:T(8,128)} %fusion.114, s32[1152]{0:T(1024)} %copy-done.83, f32[1217,768]{1,0:T(8,128)} %pad_convert_fusion, s32[2048]{0:T(1024)S(1)} %copy-done.82), kind=kCustom, calls=%fused_computation.60 | custom fusion | flops 884736 | bytes 1769472 | tf_op jit(solution)/shard_map/scatter-add | solution.py:457
  583.5 15.7 %scatter_custom_fusion.1 = f32[576,768]{1,0:T(8,128)S(1)} fusion(f32[576,768]{1,0:T(8,128)S(1)} %copy-done.16, s32[1152]{0:T(1024)} %copy-done.83, f32[1152,768]{1,0:T(8,128)} %gather_fusion.3, f32[1152]{0:T(1024)S(1)} %convert_multiply_fusion.1), kind=kCustom, calls=%fused_computation.65 | custom fusion | flops 1769472 | bytes 5316608 | tf_op jit(solution)/shard_map/scatter-add | solution.py:421
  611.5 12.4 %convert_reduce_fusion.1 = (f32[12,64]{1,0:T(8,128)S(1)}, bf16[12,64,576]{2,1,0:T(8,128)(2,1)}) fusion(bf16[576,12,64]{0,2,1:T(8,128)(2,1)} %bitcast.307, f32[12,576,576]{1,2,0:T(8,128)} %get-tuple-element.133, f32[12,576]{1,0:T(8,128)S(1)} %copy-done.48, pred[576,576]{0,1:T(8,128)(4,1)S(1)} %copy-done.25), kind=kOutput, calls=%fused_computation.80 | convolution fusion | flops 526859520 | bytes 18057216 | tf_op jit(solution)/shard_map/hqk,qhd->khd/dot_general | solution.py:494
  624.0 13.1 %multiply_reduce_fusion = (f32[12,576]{1,0:T(8,128)S(1)}, f32[12,576,576]{1,2,0:T(8,128)}) fusion(f32[12,576,576]{1,2,0:T(8,128)} %get-tuple-element.133, f32[12,576]{1,0:T(8,128)S(1)} %copy-done.48, pred[576,576]{0,1:T(8,128)(4,1)S(1)} %copy-done.25, bf16[576,12,64]{0,2,1:T(8,128)(2,1)} %bitcast.308, bf16[576,12,64]{0,2,1:T(8,128)(2,1)S(1)} %bitcast.306), kind=kOutput, calls=%fused_computation.24 | convolution fusion | flops 529507584 | bytes 34007040 | tf_op jit(solution)/shard_map/qhd,khd->hqk/dot_general | solution.py:491
  637.1 13.1 %multiply_convert_fusion = bf16[12,576,576]{1,2,0:T(8,128)(2,1)S(1)} fusion(f32[12,576,576]{1,2,0:T(8,128)} %get-tuple-element.140, f32[12,576,576]{1,2,0:T(8,128)} %get-tuple-element.133, f32[12,576]{1,0:T(8,128)S(1)} %get-tuple-element.139, f32[12,576]{1,0:T(8,128)S(1)} %copy-done.48, pred[576,576]{0,1:T(8,128)(4,1)S(1)} %copy-done.25), kind=kLoop, calls=%fused_computation.23 | loop fusion | flops 23887872 | bytes 40200192 | tf_op jit(solution)/shard_map/convert_element_type | solution.py:502
  654.1 6.6 multiply_convert_fusion.1
  686.1 54.3 %shard_map.350 = (f32[24,768]{1,0:T(8,128)}, f32[24,768]{1,0:T(8,128)}, f32[24,768]{1,0:T(8,128)}, f32[24,768]{1,0:T(8,128)}, f32[16,128]{1,0:T(8,128)}) custom-call(f32[2,2,2,2,2,24,768]{6,5,4,3,2,1,0:T(8,128)} %fusion.117.refs_0_, f32[2,2,2,2,2,24,768]{6,5,4,3,2,1,0:T(8,128)} %fusion.118.refs_1_, f32[2,2,2,2,2,24,768]{6,5,4,3,2,1,0:T(8,128)} %fusion.119.refs_2_, ...), custom_call_target="tpu_custom_call" | custom-call | tf_op jit(solution)/shard_map/pallas_call | solution.py:186
  745.2 7.1 convert_element_type.318
  752.3 76.4 %reduce-scatter.8.cloned.1.call-done = bf16[4,768,768]{2,1,0:T(8,128)(2,1)} async-done(((bf16[4,3072,768]{2,1,0:T(8,128)(2,1)}), bf16[4,768,768]{2,1,0:T(8,128)(2,1)}) %reduce-scatter.8.cloned.1.call-update) | async-done | bytes 4718608 | tf_op jit(solution)/shard_map/reduce_scatter | solution.py:468
  828.7 6.9 convert_element_type.321
  (369 shorter events, 167.2 us)
Async XLA Ops:
  13.5 102.6 %copy-start.51 = (s32[1152]{0:T(1024)}, s32[1152]{0:T(1024)S(1)}, u32[]{:S(2)}) copy-start(s32[1152]{0:T(1024)S(1)} %mul.267) | copy-start | bytes 13828
  13.7 14.9 %copy-start.2 = (bf16[24,768]{1,0:T(8,128)(2,1)S(1)}, bf16[24,768]{1,0:T(8,128)(2,1)}, u32[]{:S(2)}) copy-start(bf16[24,768]{1,0:T(8,128)(2,1)} %refs_0_.1) | copy-start | bytes 110596
  13.7 14.9 %copy-start.3 = (bf16[24,768]{1,0:T(8,128)(2,1)S(1)}, bf16[24,768]{1,0:T(8,128)(2,1)}, u32[]{:S(2)}) copy-start(bf16[24,768]{1,0:T(8,128)(2,1)} %refs_1_.1) | copy-start | bytes 110596
  13.8 14.9 %copy-start.4 = (bf16[24,768]{1,0:T(8,128)(2,1)S(1)}, bf16[24,768]{1,0:T(8,128)(2,1)}, u32[]{:S(2)}) copy-start(bf16[24,768]{1,0:T(8,128)(2,1)} %refs_2_.1) | copy-start | bytes 110596
  17.4 61.7 %copy-start.53 = (f32[576]{0:T(1024)}, f32[576]{0:T(1024)S(1)}, u32[]{:S(2)}) copy-start(f32[576]{0:T(1024)S(1)} %broadcast_multiply_fusion.1) | copy-start | bytes 6916
  17.8 50.8 %copy-start.78 = (f32[576]{0:T(1024)}, f32[576]{0:T(1024)S(1)}, u32[]{:S(2)}) copy-start(f32[576]{0:T(1024)S(1)} %fusion.60) | copy-start | bytes 6916
  17.9 61.2 %copy-start.74 = (f32[576]{0:T(1024)}, f32[576]{0:T(1024)S(1)}, u32[]{:S(2)}) copy-start(f32[576]{0:T(1024)S(1)} %fusion.91) | copy-start | bytes 6916
  70.2 48.4 %copy-start.63 = (f32[768]{0:T(1024)}, f32[768]{0:T(1024)S(1)}, u32[]{:S(2)}) copy-start(f32[768]{0:T(1024)S(1)} %reshape.656) | copy-start | bytes 9220
  83.2 20.2 %copy-start.24 = (pred[576,576]{0,1:T(8,128)(4,1)}, pred[576,576]{0,1:T(8,128)(4,1)S(1)}, u32[]{:S(2)}) copy-start(pred[576,576]{0,1:T(8,128)(4,1)S(1)} %fusion.72) | copy-start | bytes 995332
  117.4 22.3 %copy-start.84 = (s32[1152]{0:T(1024)}, s32[1152]{0:T(1024)S(1)}, u32[]{:S(2)}) copy-start(s32[1152]{0:T(1024)S(1)} %get-tuple-element.101) | copy-start | bytes 13828
  119.0 152.7 %copy-start.28 = (bf16[576,768]{1,0:T(8,128)(2,1)}, bf16[576,768]{1,0:T(8,128)(2,1)S(1)}, u32[]{:S(2)}) copy-start(bf16[576,768]{1,0:T(8,128)(2,1)S(1)} %add_convert_fusion) | copy-start | bytes 2654212
  145.6 48.6 %all-to-all-start = ((bf16[8,4,38,768]{3,1,2,0:T(4,128)(2,1)}), bf16[8,4,38,768]{3,1,2,0:T(4,128)(2,1)S(1)}, u32[]{:S(2)}, u32[]{:S(2)}) async-start(bf16[8,4,38,768]{3,1,2,0:T(4,128)(2,1)} %copy.130), calls=%async_computation | async-start | bytes 3735552 | tf_op jit(solution)/shard_map/all_to_all | solution.py:398
  150.1 87.6 %copy-start.70 = (f32[4,3072]{1,0:T(4,128)}, f32[4,3072]{1,0:T(4,128)S(1)}, u32[]{:S(2)}) copy-start(f32[4,3072]{1,0:T(4,128)S(1)} %convert_element_type.284) | copy-start | bytes 147460
  194.2 43.5 %copy-start.34 = (bf16[8,4,38,768]{3,1,2,0:T(4,128)(2,1)}, bf16[8,4,38,768]{3,1,2,0:T(4,128)(2,1)S(1)}, u32[]{:S(2)}) copy-start(bf16[8,4,38,768]{3,1,2,0:T(4,128)(2,1)S(1)} %all-to-all-done) | copy-start | bytes 5603332
  253.8 48.5 %all-to-all-start.1 = ((bf16[8,4,38,768]{3,1,2,0:T(4,128)(2,1)}), bf16[8,4,38,768]{3,1,2,0:T(4,128)(2,1)}, u32[]{:S(2)}, u32[]{:S(2)}) async-start(bf16[8,4,38,768]{3,1,2,0:T(4,128)(2,1)} %copy.132), calls=%async_computation.1 | async-start | bytes 3735552 | tf_op jit(solution)/shard_map/all_to_all | solution.py:405
  258.1 254.4 %reduce-scatter.10.cloned.1.call-start = ((), (), s32[]{:S(2)}) async-start(), calls=%async_computation.9 | async-start | bytes 983040
  368.7 47.3 %copy-start.71 = (f32[4,3072]{1,0:T(4,128)S(1)}, f32[4,3072]{1,0:T(4,128)}, u32[]{:S(2)}) copy-start(f32[4,3072]{1,0:T(4,128)} %copy-done.70) | copy-start | bytes 147460
  416.0 22.4 %copy-start.36 = (bf16[8,4,38,768]{3,1,2,0:T(4,128)(2,1)}, bf16[8,4,38,768]{3,1,2,0:T(4,128)(2,1)S(1)}, u32[]{:S(2)}) copy-start(bf16[8,4,38,768]{3,1,2,0:T(4,128)(2,1)S(1)} %all_to_all.20) | copy-start | bytes 5603332
  416.0 23.7 %copy-start.35 = (bf16[8,4,38,768]{3,1,2,0:T(4,128)(2,1)S(1)}, bf16[8,4,38,768]{3,1,2,0:T(4,128)(2,1)}, u32[]{:S(2)}) copy-start(bf16[8,4,38,768]{3,1,2,0:T(4,128)(2,1)} %copy-done.34) | copy-start | bytes 5603332
  439.7 305.5 %reduce-scatter.6.cloned.1.call-start = ((), (), s32[]{:S(2)}) async-start(), calls=%async_computation.7 | async-start | bytes 23592960 | tf_op jit(solution)/shard_map/reduce_scatter | solution.py:462
  456.4 372.2 %reduce-scatter.8.cloned.1.call-start = ((), (), s32[]{:S(2)}) async-start(), calls=%async_computation.8 | async-start | bytes 23592960 | tf_op jit(solution)/shard_map/reduce_scatter | solution.py:468
  493.0 48.9 %all-to-all-start.3 = ((bf16[8,4,38,768]{3,1,2,0:T(4,128)(2,1)}), bf16[8,4,38,768]{3,1,2,0:T(4,128)(2,1)}, u32[]{:S(2)}, u32[]{:S(2)}) async-start(bf16[8,4,38,768]{3,1,2,0:T(4,128)(2,1)} %copy.138), calls=%async_computation.3 | async-start | bytes 3735552 | tf_op jit(solution)/shard_map/all_to_all | solution.py:446
  545.2 34.2 %copy-start.16 = (f32[576,768]{1,0:T(8,128)S(1)}, f32[576,768]{1,0:T(8,128)}, u32[]{:S(2)}) copy-start(f32[576,768]{1,0:T(8,128)} %copy-done.15) | copy-start | bytes 5308420
  545.2 34.2 %copy-start.56 = (f32[576]{0:T(1024)S(1)}, f32[576]{0:T(1024)}, u32[]{:S(2)}) copy-start(f32[576]{0:T(1024)} %copy-done.55) | copy-start | bytes 6916
  545.2 34.2 %copy-start.64 = (f32[768]{0:T(1024)S(1)}, f32[768]{0:T(1024)}, u32[]{:S(2)}) copy-start(f32[768]{0:T(1024)} %copy-done.63) | copy-start | bytes 9220
  545.2 34.2 %copy-start.66 = (f32[576]{0:T(1024)S(1)}, f32[576]{0:T(1024)}, u32[]{:S(2)}) copy-start(f32[576]{0:T(1024)} %copy-done.65) | copy-start | bytes 6916
  549.0 32.7 %copy-start.81 = (f32[576]{0:T(1024)S(1)}, f32[576]{0:T(1024)}, u32[]{:S(2)}) copy-start(f32[576]{0:T(1024)} %copy-done.80) | copy-start | bytes 6916
  583.5 22.6 %copy-start.13 = (bf16[2,2,2,2,2,24,768]{6,5,4,3,2,1,0:T(8,128)(2,1)S(1)}, bf16[2,2,2,2,2,24,768]{6,5,4,3,2,1,0:T(8,128)(2,1)}, u32[]{:S(2)}) copy-start(bf16[2,2,2,2,2,24,768]{6,5,4,3,2,1,0:T(8,128)(2,1)} %copy-done.11) | copy-start | bytes 3538948
  752.3 83.3 %copy-start.60 = (f32[24,768]{1,0:T(8,128)S(1)}, f32[24,768]{1,0:T(8,128)}, u32[]{:S(2)}) copy-start(f32[24,768]{1,0:T(8,128)} %get-tuple-element.172) | copy-start | bytes 221188
  752.3 83.9 %copy-start.59 = (f32[24,768]{1,0:T(8,128)S(1)}, f32[24,768]{1,0:T(8,128)}, u32[]{:S(2)}) copy-start(f32[24,768]{1,0:T(8,128)} %get-tuple-element.174) | copy-start | bytes 221188
  752.3 84.6 %copy-start.58 = (f32[24,768]{1,0:T(8,128)S(1)}, f32[24,768]{1,0:T(8,128)}, u32[]{:S(2)}) copy-start(f32[24,768]{1,0:T(8,128)} %get-tuple-element.175) | copy-start | bytes 221188
  752.3 85.2 %copy-start.57 = (f32[24,768]{1,0:T(8,128)S(1)}, f32[24,768]{1,0:T(8,128)}, u32[]{:S(2)}) copy-start(f32[24,768]{1,0:T(8,128)} %get-tuple-element.177) | copy-start | bytes 221188
  (80 other events, 384.1 us)
Sparse Core Ops, SparseCore 0:
  439.8 24.5 reduce-scatter.9
  467.5 170.7 reduce-scatter.5
  641.7 186.8 reduce-scatter.7

commit v2 on v1

--- a/solution.py
+++ b/solution.py
@@ -254,48 +254,284 @@
     at += per * wide
     return got, weights, routers, small[at : at + rows * per].reshape(rows, per)
 
+def normal_parts(v):
+    e = jnp.exp(v * v * -0.5)
+    t = 1.0 / (1.0 + (0.3275911 * 0.7071067811865476) * jnp.abs(v))
+    poly = t * (0.127414796 + t * (-0.142248368 + t * (0.7107068705 + t * (-0.7265760135 + t * 0.5307027145))))
+    q = poly * e
+    return jnp.where(v < 0, q, 1.0 - q), e * 0.3989422804014327
+
+def dot(a, b, ca, cb):
+    return lax.dot_general(a, b, (((ca,), (cb,)), ((), ())), preferred_element_type=jnp.float32)
+
+def experts_kernel(reps, groups, compute, x_ref, g_ref, win_ref, bias_ref, wout_ref,
+                   res_ref, ig_ref, gin_ref, gb_ref, gout_ref,
+                   x_all, g_all, res_send, ig_send, wi, wo, wis, wos, act_all, pg_all, gin_buf, gout_buf, res_acc, ig_acc,
+                   own_sem, dsem, drec, rsem, rrec, bsem, brec, bown, wsem, ssem, osem):
+    me, rep = lax.axis_index("exp"), lax.axis_index("rep")
+    blocks = x_ref.shape[1]
+    cap, wide = x_ref.shape[2:]
+    rows = groups * cap
+    chunks, part = wi.shape[0], wi.shape[2]
+    half = groups // 2
+    peers = [lax.rem(me + s, groups) for s in range(1, groups)]
+    side = (rep + 1 - 2 * (rep % 2), rep + 2 - 4 * ((rep // 2) % 2))
+    both = ((x_ref, x_all), (g_ref, g_all))
+    back = ((res_send, res_ref), (ig_send, ig_ref))
+
+    def load(j, f):
+        return (pltpu.make_async_copy(win_ref.at[j, :, pl.ds(f * part, part)], wi.at[f], wsem.at[0, f]),
+                pltpu.make_async_copy(wout_ref.at[j, pl.ds(f * part, part)], wo.at[f], wsem.at[1, f]))
+    def load_slice(j):
+        at = pl.ds(pl.multiple_of(rep * part, part), part)
+        return (pltpu.make_async_copy(win_ref.at[j, :, at], wis, ssem.at[0]),
+                pltpu.make_async_copy(wout_ref.at[j, at], wos, ssem.at[1]))
+    def out_copies(j):
+        return (pltpu.make_async_copy(gin_buf, gin_ref.at[j], osem.at[0]),
+                pltpu.make_async_copy(gout_buf, gout_ref.at[j], osem.at[1]))
+    def dispatch(j, t, s):
+        src, dst = both[t]
+        return pltpu.make_async_remote_copy(src.at[peers[s], j], dst.at[j, 0, me], dsem.at[t, j, s], drec.at[t, j, s],
+                                            device_id=(rep, peers[s]), device_id_type=MESH)
+    def own(j, t):
+        src, dst = both[t]
+        return pltpu.make_async_copy(src.at[me, j], dst.at[j, 0, me], own_sem.at[t, j])
+    def across(j, t, n):
+        dst = both[t][1]
+        return pltpu.make_async_remote_copy(dst.at[j, 0], dst.at[j, 1 + n], rsem.at[t, j, n], rrec.at[t, j, n],
+                                            device_id=(side[n], me), device_id_type=MESH)
+    def onward(j, t, n):
+        dst = both[t][1]
+        at = pl.ds(n * half, half)
+        return pltpu.make_async_remote_copy(dst.at[j, 1 + n, at], dst.at[j, 3, at], rsem.at[t, j, 2 + n], rrec.at[t, j, 2 + n],
+                                            device_id=(side[1 - n], me), device_id_type=MESH)
+    def give(j, t, s):
+        src, dst = back[t]
+        return pltpu.make_async_remote_copy(src.at[j, peers[s]], dst.at[me, j], bsem.at[t, j, s], brec.at[t, j, s],
+                                            device_id=(rep, peers[s]), device_id_type=MESH)
+    def give_own(j, t):
+        src, dst = back[t]
+        return pltpu.make_async_copy(src.at[j, me], dst.at[me, j], bown.at[t, j])
+    def flat(v):
+        return v.astype(jnp.float32).reshape(-1, wide).astype(jnp.bfloat16)
+
+    barrier = pltpu.get_barrier_semaphore()
+    for p in peers:
+        pl.semaphore_signal(barrier, inc=1, device_id=(rep, p), device_id_type=MESH)
+    for n in side:
+        pl.semaphore_signal(barrier, inc=1, device_id=(n, me), device_id_type=MESH)
+    pl.semaphore_wait(barrier, groups - 1 + 2)
+
+    def send_all(j, _):
+        for t in range(2):
+            for s in range(groups - 1):
+                dispatch(j, t, s).start()
+            own(j, t).start()
+        return 0
+    lax.fori_loop(0, blocks, send_all, 0)
+    if compute:
+        for f in range(chunks):
+            for c in load(0, f): c.start()
+        for c in load_slice(0): c.start()
+
+    def own_rows(j):
+        x, g = flat(x_all[j, 0]), flat(g_all[j, 0])
+        def chunk(f, _):
+            for c in load(j, f): c.wait()
+            pre = dot(x, wi[f], 1, 0) + bias_ref[j, f]
+            cdf, pdf = normal_parts(pre)
+            act = (pre * cdf).astype(jnp.bfloat16)
+            ag = dot(g, wo[f], 1, 1)
+            pg = (ag * (cdf + pre * pdf)).astype(jnp.bfloat16)
+            more, less = dot(act, wo[f], 1, 0), dot(pg, wi[f], 1, 1)
+            @pl.when(f == 0)
+            def _():
+                res_acc[...] = more
+                ig_acc[...] = less
+            @pl.when(f > 0)
+            def _():
+                res_acc[...] += more
+                ig_acc[...] += less
+            @pl.when(j + 1 < blocks)
+            def _():
+                for c in load(j + 1, f): c.start()
+            return 0
+        lax.fori_loop(0, chunks, chunk, 0)
+        res_send[j] = res_acc[...].reshape(groups, cap, wide).astype(jnp.bfloat16)
+        ig_send[j] = ig_acc[...].reshape(groups, cap, wide).astype(jnp.bfloat16)
+
+    def weights(j):
+        for c in load_slice(j): c.wait()
+        def one(r, _):
+            x, g = flat(x_all[j, r]), flat(g_all[j, r])
+            pre = dot(x, wis[...], 1, 0) + bias_ref[j, rep]
+            cdf, pdf = normal_parts(pre)
+            act_all[r] = (pre * cdf).astype(jnp.bfloat16)
+            pg_all[r] = (dot(g, wos[...], 1, 1) * (cdf + pre * pdf)).astype(jnp.bfloat16)
+            return 0
+        lax.fori_loop(0, reps, one, 0)
+        @pl.when(j + 1 < blocks)
+        def _():
+            for c in load_slice(j + 1): c.start()
+        @pl.when(j > 0)
+        def _():
+            for c in out_copies(j - 1): c.wait()
+        act, pg = act_all[...].reshape(reps * rows, part), pg_all[...].reshape(reps * rows, part)
+        gout_buf[...] = dot(act, flat(g_all[j]), 0, 0)
+        gin_buf[...] = dot(flat(x_all[j]), pg, 0, 0)
+        gb_ref[j] = jnp.sum(pg.astype(jnp.float32), axis=0, keepdims=True)
+        for c in out_copies(j): c.start()
+
+    def step(k, _):
+        @pl.when(k < blocks)
+        def _():
+            for t in range(2):
+                for s in range(groups - 1):
+                    dispatch(k, t, s).wait_recv()
+                own(k, t).wait()
+                for n in range(2):
+                    across(k, t, n).start()
+            if compute:
+                own_rows(k)
+            else:
+                res_send[k] = x_all[k, 0]
+                ig_send[k] = g_all[k, 0]
+            for t in range(2):
+                for s in range(groups - 1):
+                    give(k, t, s).start()
+                give_own(k, t).start()
+        @pl.when((k > 0) & (k <= blocks))
+        def _():
+            for t in range(2):
+                for n in range(2):
+                    across(k - 1, t, n).wait_recv()
+                for n in range(2):
+                    onward(k - 1, t, n).start()
+        @pl.when(k > 1)
+        def _():
+            for t in range(2):
+                for n in range(2):
+                    onward(k - 2, t, n).wait_recv()
+            if compute:
+                weights(k - 2)
+        return 0
+    lax.fori_loop(0, blocks + 2, step, 0)
+
+    if compute:
+        for c in out_copies(blocks - 1): c.wait()
+    def drain(j, _):
+        for t in range(2):
+            for s in range(groups - 1):
+                give(j, t, s).wait_recv()
+                give(j, t, s).wait_send()
+                dispatch(j, t, s).wait_send()
+            give_own(j, t).wait()
+            for n in range(2):
+                across(j, t, n).wait_send()
+                onward(j, t, n).wait_send()
+        return 0
+    lax.fori_loop(0, blocks, drain, 0)
+
+
+def experts_call(x, g, w_in, b_in, w_out, reps, groups, compute=True):
+    _, blocks, cap, wide = x.shape
+    hidden = w_in.shape[2]
+    part = hidden // reps
+    bias = b_in.astype(jnp.float32).reshape(blocks, reps, 1, part)
+    anyw = pl.BlockSpec(memory_space=pl.ANY)
+    vm = pl.BlockSpec(memory_space=pltpu.VMEM)
+    bf, f32 = jnp.bfloat16, jnp.float32
+    sem = pltpu.SemaphoreType.DMA
+    n = groups - 1
+    rows = groups * cap
+    return pl.pallas_call(
+        functools.partial(experts_kernel, reps, groups, compute),
+        out_shape=[jax.ShapeDtypeStruct(x.shape, bf), jax.ShapeDtypeStruct(x.shape, bf),
+                   jax.ShapeDtypeStruct((blocks, wide, part), f32), jax.ShapeDtypeStruct((blocks, 1, part), f32),
+                   jax.ShapeDtypeStruct((blocks, part, wide), f32)],
+        in_specs=[anyw, anyw, anyw, vm, anyw],
+        out_specs=[anyw, anyw, anyw, vm, anyw],
+        scratch_shapes=[
+            pltpu.VMEM((blocks, reps, groups, cap, wide), bf), pltpu.VMEM((blocks, reps, groups, cap, wide), bf),
+            pltpu.VMEM((blocks, groups, cap, wide), bf), pltpu.VMEM((blocks, groups, cap, wide), bf),
+            pltpu.VMEM((reps, wide, part), bf), pltpu.VMEM((reps, part, wide), bf),
+            pltpu.VMEM((wide, part), bf), pltpu.VMEM((part, wide), bf),
+            pltpu.VMEM((reps, rows, part), bf), pltpu.VMEM((reps, rows, part), bf),
+            pltpu.VMEM((wide, part), f32), pltpu.VMEM((part, wide), f32),
+            pltpu.VMEM((rows, wide), f32), pltpu.VMEM((rows, wide), f32),
+            sem((2, blocks)), sem((2, blocks, n)), sem((2, blocks, n)), sem((2, blocks, 4)), sem((2, blocks, 4)),
+            sem((2, blocks, n)), sem((2, blocks, n)), sem((2, blocks)), sem((2, reps)), sem((2,)), sem((2,))],
+        compiler_params=pltpu.CompilerParams(collective_id=2, has_side_effects=True, vmem_limit_bytes=60 * MIB),
+    )(x, g, w_in, bias, w_out)
+
+def experts_plain(x, g, w_in, b_in, w_out):
+    bf, f32 = jnp.bfloat16, jnp.float32
+    rx = lax.all_to_all(x, "exp", split_axis=0, concat_axis=0, tiled=True)
+    rg = lax.all_to_all(g, "exp", split_axis=0, concat_axis=0, tiled=True)
+    pre = jnp.einsum("secd,edf->secf", rx, w_in, preferred_element_type=f32)
+    pre = pre + b_in.astype(f32)[None, :, None, :]
+    cdf, pdf = normal_parts(pre)
+    act = (pre * cdf).astype(bf)
+    res = jnp.einsum("secf,efd->secd", act, w_out, preferred_element_type=f32).astype(bf)
+    pg = jnp.einsum("secd,efd->secf", rg, w_out, preferred_element_type=f32) * (cdf + pre * pdf)
+    pg = pg.astype(bf)
+    ig = jnp.einsum("secf,edf->secd", pg, w_in, preferred_element_type=f32).astype(bf)
+    gout = jnp.einsum("secf,secd->efd", act, rg, preferred_element_type=f32).astype(bf)
+    gin = jnp.einsum("secd,secf->edf", rx, pg, preferred_element_type=f32).astype(bf)
+    gb = jnp.sum(pg, axis=(0, 2), dtype=f32).astype(bf)
+    return (
+        lax.all_to_all(res, "exp", split_axis=0, concat_axis=0, tiled=True),
+        lax.all_to_all(ig, "exp", split_axis=0, concat_axis=0, tiled=True),
+        lax.psum_scatter(gin, "rep", scatter_dimension=2, tiled=True).astype(f32),
+        lax.psum_scatter(gb, "rep", scatter_dimension=1, tiled=True).astype(f32)[:, None],
+        lax.psum_scatter(gout, "rep", scatter_dimension=1, tiled=True).astype(f32),
+    )
+
 
 epsilon = 1e-06
 masked_score = -1e30
 
 
-def layer_norm(values, gain, bias):
+def normalize(values):
     center = values - jnp.mean(values, axis=-1, keepdims=True)
     spread = jnp.mean(center * center, axis=-1, keepdims=True)
-    return center * lax.rsqrt(spread + epsilon) * gain + bias
-
-
-def slot_table(row_routes, row_priority, valid_mask, experts, capacity):
-    top_count = row_routes.shape[1]
-    chosen = row_routes[row_priority]
-    seq_expert = jnp.transpose(chosen).reshape(-1)
-    seq_token = jnp.tile(row_priority, top_count)
-    seq_valid = jnp.tile(valid_mask[row_priority], top_count)
-    expert_ids = jnp.arange(experts, dtype=jnp.int32)
-    onehot = (seq_expert[:, None] == expert_ids[None, :]).astype(jnp.int32) * seq_valid[:, None]
-    before = jnp.cumsum(onehot, axis=0, dtype=jnp.int32) - onehot
-    position = jnp.sum(before * onehot, axis=1, dtype=jnp.int32)
-    kept_mask = seq_valid * (position < capacity).astype(jnp.int32)
-    slot_id = jnp.where(kept_mask > 0, seq_expert * capacity + position, experts * capacity)
-    return (seq_token, seq_expert, slot_id, kept_mask)
-
-
-def attention_probs(query_heads, key_heads, allowed, score_scale, log_total):
-    scores = (
-        jnp.einsum("qhd,khd->hqk", query_heads, key_heads, preferred_element_type=jnp.float32)
-        * score_scale
-    )
-    masked = jnp.where(allowed[None], scores, masked_score)
-    if log_total is None:
-        top_score = jnp.max(masked, axis=-1, keepdims=True)
-        log_total = top_score + jnp.log(
-            jnp.sum(jnp.exp(masked - top_score), axis=-1, keepdims=True)
-        )
-    return (jnp.exp(masked - log_total), log_total)
-
-
-def gelu_exact(values):
-    return jax.nn.gelu(values, approximate=False)
+    scale = lax.rsqrt(spread + epsilon)
+    return center * scale, scale
+
+
+def normalize_back(grad, unit, scale):
+    mean = jnp.mean(grad, axis=-1, keepdims=True)
+    along = jnp.mean(grad * unit, axis=-1, keepdims=True)
+    return (grad - mean - unit * along) * scale
+
+
+def two_parts(v):
+    high = v.astype(jnp.bfloat16)
+    return high, (v - high.astype(jnp.float32)).astype(jnp.bfloat16)
+
+
+def positions_of(routes, valid_col, priority_col, priority_row, experts):
+    length = routes.shape[0]
+    f32, bf = jnp.float32, jnp.bfloat16
+    token_row = lax.broadcasted_iota(jnp.int32, (length, length), 1)
+    token_col = lax.broadcasted_iota(jnp.int32, (length, length), 0)
+    rank_col = jnp.sum(
+        jnp.where(priority_row == token_col, token_row, 0).astype(f32), axis=1, keepdims=True
+    )
+    rank_row = jnp.sum(
+        jnp.where(priority_col == token_row, token_col, 0).astype(f32), axis=0, keepdims=True
+    )
+    earlier = (rank_row < rank_col).astype(f32).astype(bf)
+    expert_row = lax.broadcasted_iota(jnp.int32, (length, experts), 1)
+    ones = [(routes[:, k : k + 1] == expert_row).astype(f32) for k in range(routes.shape[1])]
+    before = jnp.zeros((1, experts), f32)
+    places = []
+    for one in ones:
+        live = one * valid_col
+        count = dot(earlier, live.astype(bf), 1, 0) + before
+        places.append(jnp.sum(count * one, axis=1, keepdims=True))
+        before = before + jnp.sum(live, axis=0, keepdims=True)
+    return ones, places
 
 
 def body(
@@ -322,213 +558,156 @@
     expert_out_bias,
     cotangent,
 ):
+    f32, bf = jnp.float32, jnp.bfloat16
     vectors, weights, router_weight, result_shift = gather_all(
         [ln1_gain, ln1_bias, query_bias, value_bias, attn_out_bias, ln2_gain, ln2_bias],
         [w_query, w_key, w_value, w_attn_out],
         w_router,
         expert_out_bias,
     )
+    vectors = [v.astype(f32)[None] for v in vectors]
     gain_one, bias_one, query_shift, value_shift, proj_shift, gain_two, bias_two = vectors
     query_weight, key_weight, value_weight, proj_weight = weights
-    gain_one = gain_one.astype(jnp.float32)
-    bias_one = bias_one.astype(jnp.float32)
-    gain_two = gain_two.astype(jnp.float32)
-    bias_two = bias_two.astype(jnp.float32)
     length = tokens.shape[1]
     feature_dim = tokens.shape[2]
-    head_count = HEADS
-    head_dim = feature_dim // head_count
+    head_dim = feature_dim // HEADS
     local_blocks = expert_in.shape[0]
-    groups = lax.axis_size("exp")
+    reps, groups = lax.axis_size("rep"), lax.axis_size("exp")
     experts = EXPERTS
     split = local_blocks * groups // experts
     top_count = routes.shape[2]
     capacity = (105 * top_count * length + 100 * experts - 1) // (100 * experts)
+    room = -(-capacity // 8) * 8
     score_scale = head_dim ** (-0.5)
-    inputs = tokens[0].astype(jnp.float32)
+    inputs = tokens[0].astype(f32)
     row_segments = segments[0]
     row_valid = valid[0]
-    positions = jnp.arange(length, dtype=jnp.int32)
+    places = jnp.arange(length, dtype=jnp.int32)
     allowed = (row_segments[:, None] == row_segments[None, :]) & (
-        (row_valid[None, :] > 0) | (positions[:, None] == positions[None, :])
-    )
-    normed = layer_norm(inputs, gain_one, bias_one).astype(jnp.bfloat16)
-    query_rows = (
-        jnp.dot(normed, query_weight, preferred_element_type=jnp.float32)
-        + query_shift.astype(jnp.float32)
-    ).astype(jnp.bfloat16)
-    key_rows = jnp.dot(normed, key_weight, preferred_element_type=jnp.float32).astype(jnp.bfloat16)
-    value_rows = (
-        jnp.dot(normed, value_weight, preferred_element_type=jnp.float32)
-        + value_shift.astype(jnp.float32)
-    ).astype(jnp.bfloat16)
-    query_heads = query_rows.reshape(length, head_count, head_dim)
-    key_heads = key_rows.reshape(length, head_count, head_dim)
-    value_heads = value_rows.reshape(length, head_count, head_dim)
-    attn_weights, log_total = attention_probs(query_heads, key_heads, allowed, score_scale, None)
+        (row_valid[None, :] > 0) | (places[:, None] == places[None, :])
+    )
+    unit_one, scale_one = normalize(inputs)
+    normed = (unit_one * gain_one + bias_one).astype(bf)
+    query_rows = (dot(normed, query_weight, 1, 0) + query_shift).astype(bf)
+    key_rows = dot(normed, key_weight, 1, 0).astype(bf)
+    value_rows = (dot(normed, value_weight, 1, 0) + value_shift).astype(bf)
+    query_heads = query_rows.reshape(length, HEADS, head_dim)
+    key_heads = key_rows.reshape(length, HEADS, head_dim)
+    value_heads = value_rows.reshape(length, HEADS, head_dim)
+
+    def scores():
+        return jnp.where(
+            allowed[None],
+            jnp.einsum("qhd,khd->hqk", query_heads, key_heads, preferred_element_type=f32)
+            * score_scale,
+            masked_score,
+        )
+
+    masked = scores()
+    top_score = jnp.max(masked, axis=-1, keepdims=True)
+    log_total = top_score + jnp.log(jnp.sum(jnp.exp(masked - top_score), axis=-1, keepdims=True))
     mixed = jnp.einsum(
         "hqk,khd->qhd",
-        attn_weights.astype(jnp.bfloat16),
+        jnp.exp(masked - log_total).astype(bf),
         value_heads,
-        preferred_element_type=jnp.float32,
-    )
-    mixed = mixed.reshape(length, feature_dim).astype(jnp.bfloat16)
-    residual = (
-        inputs
-        + jnp.dot(mixed, proj_weight, preferred_element_type=jnp.float32)
-        + proj_shift.astype(jnp.float32)
-    )
-    normed_two = layer_norm(residual, gain_two, bias_two).astype(jnp.bfloat16)
-    logits = jnp.dot(normed_two, router_weight, preferred_element_type=jnp.float32)
+        preferred_element_type=f32,
+    )
+    mixed = mixed.reshape(length, feature_dim).astype(bf)
+    residual = inputs + dot(mixed, proj_weight, 1, 0) + proj_shift
+    unit_two, scale_two = normalize(residual)
+    normed_two = (unit_two * gain_two + bias_two).astype(bf)
+    logits = dot(normed_two, router_weight, 1, 0)
     logit_exp = jnp.exp(logits - jnp.max(logits, axis=-1, keepdims=True))
     router_probs = logit_exp / jnp.sum(logit_exp, axis=-1, keepdims=True)
-    seq_token, seq_expert, slot_id, kept_mask = slot_table(
-        routes[0], priority[0], row_valid, experts, capacity
-    )
-    kept_float = kept_mask.astype(jnp.float32)
-    buffer = (
-        jnp.zeros((experts * capacity + 1, feature_dim), jnp.bfloat16)
-        .at[slot_id]
-        .add(normed_two[seq_token])
-    )
-    expert_slots = buffer[: experts * capacity].reshape(experts, capacity, feature_dim)
-    outgoing = jnp.repeat(expert_slots, split, axis=0).reshape(
-        groups, local_blocks, capacity, feature_dim
-    )
-    received = lax.all_to_all(outgoing, "exp", split_axis=0, concat_axis=0, tiled=True)
-    pre_act = (
-        jnp.einsum("secd,edf->secf", received, expert_in, preferred_element_type=jnp.float32)
-        + expert_in_bias.astype(jnp.float32)[None, :, None, :]
-    )
-    active = gelu_exact(pre_act).astype(jnp.bfloat16)
-    result = jnp.einsum("secf,efd->secd", active, expert_out, preferred_element_type=jnp.float32)
-    returned = lax.all_to_all(
-        result.astype(jnp.bfloat16), "exp", split_axis=0, concat_axis=0, tiled=True
-    )
-    summed = jnp.sum(
-        returned.reshape(experts, split, capacity, feature_dim).astype(jnp.float32), axis=1
-    )
-    summed = summed + result_shift.astype(jnp.float32)[:, None, :]
-    flat_result = jnp.concatenate(
-        [summed.reshape(experts * capacity, feature_dim), jnp.zeros((1, feature_dim), jnp.float32)],
-        axis=0,
-    )
-    picked = flat_result[slot_id]
-    gate_values = router_probs[seq_token, seq_expert] * kept_float
-    combined = (
-        jnp.zeros((length, feature_dim), jnp.float32)
-        .at[seq_token]
-        .add(gate_values[:, None] * picked)
-    )
+    upstream = cotangent[0].astype(f32)
+    ones, positions = positions_of(
+        routes[0], row_valid[:, None].astype(f32), priority[0][:, None], priority[0][None], experts
+    )
+    expert_row = lax.broadcasted_iota(jnp.int32, (1, experts), 1).astype(f32)
+    slot_row = lax.broadcasted_iota(jnp.int32, (1, experts * room), 1)
+    kept, gates, slots, sent = [], [], [], jnp.zeros((experts * room, feature_dim), f32)
+    for one, position in zip(ones, positions):
+        keep = row_valid[:, None].astype(f32) * (position < capacity).astype(f32)
+        gate = jnp.sum(router_probs * one, axis=1, keepdims=True) * keep
+        place = jnp.sum(one * expert_row, axis=1, keepdims=True) * room + position
+        place = jnp.where(keep > 0, place, -1.0).astype(jnp.int32)
+        hot = (place == slot_row).astype(f32).astype(bf)
+        kept.append(one * keep)
+        gates.append(gate)
+        slots.append(hot)
+        sent = sent + dot(hot, (gate * upstream).astype(bf), 0, 0)
+    any_slot = slots[0]
+    for hot in slots[1:]:
+        any_slot = any_slot + hot
+    expert_slots = dot(any_slot, normed_two, 0, 0).astype(bf)
+    gated = sum(one * gate for one, gate in zip(kept, gates))
+    high, low = two_parts(gated)
+    shift_grad = dot(high, cotangent[0], 0, 0) + dot(low, cotangent[0], 0, 0)
+
+    def outgoing(v):
+        v = v.astype(bf).reshape(experts, room, feature_dim)
+        return jnp.repeat(v, split, axis=0).reshape(groups, local_blocks, room, feature_dim)
+
+    small = reps == 4 and groups * room <= 512 and expert_in.shape[2] % (128 * reps) == 0
+    if small:
+        moved = experts_call(
+            outgoing(expert_slots), outgoing(sent), expert_in, expert_in_bias, expert_out, reps, groups
+        )
+    else:
+        moved = experts_plain(
+            outgoing(expert_slots), outgoing(sent), expert_in, expert_in_bias, expert_out
+        )
+    result, slot_back, in_w_grad, in_b_grad, out_w_grad = moved
+    result = result.reshape(experts, split, room, feature_dim)
+    slot_back = slot_back.reshape(experts, split, room, feature_dim)
+    results = [result[:, s].reshape(experts * room, feature_dim) for s in range(split)]
+    backs = [slot_back[:, s].reshape(experts * room, feature_dim) for s in range(split)]
+    combined, prob_grad = 0.0, 0.0
+    for one, gate, hot in zip(kept, gates, slots):
+        picked = dot(one.astype(bf), result_shift, 1, 0)
+        for part in results:
+            picked = picked + dot(hot, part, 1, 0)
+        combined = combined + gate * picked
+        prob_grad = prob_grad + one * jnp.sum(upstream * picked, axis=1, keepdims=True)
     output = residual + combined
-    upstream = cotangent[0].astype(jnp.float32)
-    token_grad = upstream[seq_token]
-    gate_grad = jnp.sum(token_grad * picked, axis=1) * kept_float
-    slot_terms = (
-        jnp.zeros((experts * capacity + 1, feature_dim), jnp.float32)
-        .at[slot_id]
-        .add(gate_values[:, None] * token_grad)
-    )
-    slot_terms = slot_terms[: experts * capacity].reshape(experts, capacity, feature_dim)
-    shift_grad = jnp.sum(slot_terms, axis=1)
-    slot_grad = jnp.repeat(slot_terms.astype(jnp.bfloat16), split, axis=0).reshape(
-        groups, local_blocks, capacity, feature_dim
-    )
-    back_grad = lax.all_to_all(slot_grad, "exp", split_axis=0, concat_axis=0, tiled=True)
-    active_grad = jnp.einsum(
-        "secd,efd->secf", back_grad, expert_out, preferred_element_type=jnp.float32
-    )
-    gelu_back = jax.vjp(gelu_exact, pre_act)[1]
-    pre_grad = gelu_back(active_grad)[0].astype(jnp.bfloat16)
-    slot_input_grad = jnp.einsum(
-        "secf,edf->secd", pre_grad, expert_in, preferred_element_type=jnp.float32
-    ).astype(jnp.bfloat16)
-    sent_back = lax.all_to_all(slot_input_grad, "exp", split_axis=0, concat_axis=0, tiled=True)
-    back_sum = jnp.sum(
-        sent_back.reshape(experts, split, capacity, feature_dim).astype(jnp.float32), axis=1
-    )
-    flat_back = jnp.concatenate(
-        [
-            back_sum.reshape(experts * capacity, feature_dim),
-            jnp.zeros((1, feature_dim), jnp.float32),
-        ],
-        axis=0,
-    )
-    moe_grad = jnp.zeros((length, feature_dim), jnp.float32).at[seq_token].add(flat_back[slot_id])
-    out_w_grad = jnp.einsum("secf,secd->efd", active, back_grad, preferred_element_type=jnp.float32)
-    in_w_grad = jnp.einsum("secd,secf->edf", received, pre_grad, preferred_element_type=jnp.float32)
-    in_b_grad = jnp.sum(pre_grad, axis=(0, 2), dtype=jnp.float32)
-    expert_sums = (
-        lax.psum_scatter(
-            in_w_grad.astype(jnp.bfloat16), "rep", scatter_dimension=2, tiled=True
-        ).astype(jnp.float32),
-        lax.psum_scatter(
-            in_b_grad.astype(jnp.bfloat16), "rep", scatter_dimension=1, tiled=True
-        ).astype(jnp.float32),
-        lax.psum_scatter(
-            out_w_grad.astype(jnp.bfloat16), "rep", scatter_dimension=1, tiled=True
-        ).astype(jnp.float32),
-    )
-    prob_grad = jnp.zeros((length, experts), jnp.float32).at[seq_token, seq_expert].add(gate_grad)
     logit_grad = (
         router_probs * (prob_grad - jnp.sum(router_probs * prob_grad, axis=-1, keepdims=True))
-    ).astype(jnp.bfloat16)
-    router_w_grad = jnp.dot(normed_two.T, logit_grad, preferred_element_type=jnp.float32)
-    normed_two_grad = moe_grad + jnp.dot(
-        logit_grad, router_weight.T, preferred_element_type=jnp.float32
-    )
-    norm_two_back = jax.vjp(layer_norm, residual, gain_two, bias_two)[1]
-    residual_ln_grad, gain_two_grad, bias_two_grad = norm_two_back(normed_two_grad)
-    residual_grad = upstream + residual_ln_grad
-    branch_grad = residual_grad.astype(jnp.bfloat16)
-    proj_w_grad = jnp.dot(mixed.T, branch_grad, preferred_element_type=jnp.float32)
-    proj_b_grad = jnp.sum(branch_grad, axis=0, dtype=jnp.float32)
-    mixed_grad = jnp.dot(branch_grad, proj_weight.T, preferred_element_type=jnp.float32).astype(
-        jnp.bfloat16
-    )
-    mixed_grad = mixed_grad.reshape(length, head_count, head_dim)
-    again_probs = attention_probs(query_heads, key_heads, allowed, score_scale, log_total)[0]
-    prob_grads = jnp.einsum(
-        "qhd,khd->hqk", mixed_grad, value_heads, preferred_element_type=jnp.float32
-    )
+    ).astype(bf)
+    router_w_grad = dot(normed_two, logit_grad, 0, 0)
+    normed_two_grad = dot(logit_grad, router_weight, 1, 1)
+    for part in backs:
+        normed_two_grad = normed_two_grad + dot(any_slot, part, 1, 0)
+    gain_two_grad = jnp.sum(normed_two_grad * unit_two, axis=0)
+    bias_two_grad = jnp.sum(normed_two_grad, axis=0)
+    residual_grad = upstream + normalize_back(normed_two_grad * gain_two, unit_two, scale_two)
+    branch_grad = residual_grad.astype(bf)
+    proj_w_grad = dot(mixed, branch_grad, 0, 0)
+    proj_b_grad = jnp.sum(branch_grad, axis=0, dtype=f32)
+    mixed_grad = dot(branch_grad, proj_weight, 1, 1).astype(bf)
+    mixed_grad = mixed_grad.reshape(length, HEADS, head_dim)
+    again_probs = jnp.exp(scores() - log_total)
+    prob_grads = jnp.einsum("qhd,khd->hqk", mixed_grad, value_heads, preferred_element_type=f32)
     value_grad = jnp.einsum(
-        "hqk,qhd->khd",
-        again_probs.astype(jnp.bfloat16),
-        mixed_grad,
-        preferred_element_type=jnp.float32,
-    )
-    value_grad = value_grad.astype(jnp.bfloat16).reshape(length, feature_dim)
+        "hqk,qhd->khd", again_probs.astype(bf), mixed_grad, preferred_element_type=f32
+    )
+    value_grad = value_grad.astype(bf).reshape(length, feature_dim)
     inner_sum = jnp.sum(again_probs * prob_grads, axis=-1, keepdims=True)
-    score_grad = (again_probs * (prob_grads - inner_sum)).astype(jnp.bfloat16)
-    query_grad = (
-        (
-            jnp.einsum("hqk,khd->qhd", score_grad, key_heads, preferred_element_type=jnp.float32)
-            * score_scale
-        )
-        .astype(jnp.bfloat16)
-        .reshape(length, feature_dim)
-    )
-    key_grad = (
-        (
-            jnp.einsum("hqk,qhd->khd", score_grad, query_heads, preferred_element_type=jnp.float32)
-            * score_scale
-        )
-        .astype(jnp.bfloat16)
-        .reshape(length, feature_dim)
-    )
-    query_w_grad = jnp.dot(normed.T, query_grad, preferred_element_type=jnp.float32)
-    query_b_grad = jnp.sum(query_grad, axis=0, dtype=jnp.float32)
-    key_w_grad = jnp.dot(normed.T, key_grad, preferred_element_type=jnp.float32)
-    value_w_grad = jnp.dot(normed.T, value_grad, preferred_element_type=jnp.float32)
-    value_b_grad = jnp.sum(value_grad, axis=0, dtype=jnp.float32)
-    normed_grad = jnp.dot(query_grad, query_weight.T, preferred_element_type=jnp.float32)
-    normed_grad = normed_grad + jnp.dot(key_grad, key_weight.T, preferred_element_type=jnp.float32)
-    normed_grad = normed_grad + jnp.dot(
-        value_grad, value_weight.T, preferred_element_type=jnp.float32
-    )
-    norm_one_back = jax.vjp(layer_norm, inputs, gain_one, bias_one)[1]
-    input_ln_grad, gain_one_grad, bias_one_grad = norm_one_back(normed_grad)
-    tokens_grad = residual_grad + input_ln_grad
+    score_grad = (again_probs * (prob_grads - inner_sum)).astype(bf)
+    query_grad = jnp.einsum("hqk,khd->qhd", score_grad, key_heads, preferred_element_type=f32)
+    query_grad = (query_grad * score_scale).astype(bf).reshape(length, feature_dim)
+    key_grad = jnp.einsum("hqk,qhd->khd", score_grad, query_heads, preferred_element_type=f32)
+    key_grad = (key_grad * score_scale).astype(bf).reshape(length, feature_dim)
+    query_w_grad = dot(normed, query_grad, 0, 0)
+    query_b_grad = jnp.sum(query_grad, axis=0, dtype=f32)
+    key_w_grad = dot(normed, key_grad, 0, 0)
+    value_w_grad = dot(normed, value_grad, 0, 0)
+    value_b_grad = jnp.sum(value_grad, axis=0, dtype=f32)
+    normed_grad = dot(query_grad, query_weight, 1, 1)
+    normed_grad = normed_grad + dot(key_grad, key_weight, 1, 1)
+    normed_grad = normed_grad + dot(value_grad, value_weight, 1, 1)
+    gain_one_grad = jnp.sum(normed_grad * unit_one, axis=0)
+    bias_one_grad = jnp.sum(normed_grad, axis=0)
+    tokens_grad = residual_grad + normalize_back(normed_grad * gain_one, unit_one, scale_one)
     vector_sums, weight_sums, router_sum, shift_sum = scatter_all(
         [
             gain_one_grad,
@@ -558,9 +737,9 @@
         vector_sums[5],
         vector_sums[6],
         router_sum,
-        expert_sums[0],
-        expert_sums[1],
-        expert_sums[2],
+        in_w_grad,
+        in_b_grad[:, 0],
+        out_w_grad,
         shift_sum,
     )
 

time: 852 us -> 516 us (0.61)
  waiting for transfers between devices: 178 us -> 0 us
  Pallas kernels: 92.2 us -> 260 us
  other arithmetic: 174 us -> 45 us
  matrix products: 213 us -> 119 us
  blocking collectives: 46.6 us -> 0 us
  local copies, waits for them, and re-layouts: 112 us -> 83.3 us
  starting transfers between devices: 13.7 us -> 0 us
  between operations: 15.8 us -> 2.14 us
    pallas_call x0 -> x1, Pallas kernels: none -> 176 us  [experts_call(): pl.pallas_call(functools.partial(experts_kernel, reps, groups, compute),...]
    all_to_all x3 -> x0, waiting for transfers between devices: 102 us -> none  [the longest x1 44.1 us: body(): lax.all_to_all(outgoing, 'exp', split_axis=0, concat_axis=0, tiled=True)]
    dot_general x24 -> x30, matrix products: 190 us -> 96.5 us  [the longest x27 62.8 us: dot(): lax.dot_general(a, b, (((ca,), (cb,)), ((), ())), preferred_element_type=...]
    scatter-add x4 -> x0, other arithmetic: 83.4 us -> none  [the longest x1 30.4 us: body(): jnp.zeros((length, feature_dim), jnp.float32).at[seq_token]]
    reduce_scatter x2 -> x0, waiting for transfers between devices: 76.4 us -> none  [the longest x1 76.4 us: body(): lax.psum_scatter(out_w_grad.astype(jnp.bfloat16), 'rep', scatter_dimensio...]
    all_to_all x1 -> x0, blocking collectives: 46.6 us -> none  [body(): lax.all_to_all(slot_grad, 'exp', split_axis=0, concat_axis=0, tiled=True)]
    gather x5 -> x0, local copies, waits for them, and re-layouts: 26.8 us -> none  [the longest x1 9.7 us: body(): gate_values = router_probs[seq_token, seq_expert] * kept_float]
    unnamed x225 -> x180, local copies, waits for them, and re-layouts: 15.9 us -> 36.8 us
  transfers between devices with their start and end apart: 6 -> 0, of which waited for: 4 -> 0; matrix products, arithmetic and copies ran while one was open for 28% -> 0% of each run, Pallas kernels for 6% -> 0%
where the time goes in v2:
time: 516 us; the launch traced here: 510 us
  Pallas kernels  260 us (50%)
  matrix products  119 us (23%)
  local copies, waits for them, and re-layouts  83.3 us (16%)
  other arithmetic  45 us (9%)
    pallas_call x1, Pallas kernels, experts_call(): pl.pallas_call(functools.partial(experts_kernel, reps, groups, compute),...  176 us
    dot_general x27, matrix products, dot(): lax.dot_general(a, b, (((ca,), (cb,)), ((), ())), preferred_element_type=...  62.8 us
    pallas_call x1, Pallas kernels, scatter_grads(): pl.pallas_call(functools.partial(scatter_kernel, dims, widths, count), ou...  47 us
    pallas_call x1, Pallas kernels, gather_params(): pl.pallas_call(functools.partial(gather_kernel, dims, widths, count), out...  37.8 us
    unnamed x180, local copies, waits for them, and re-layouts  36.8 us
    dot_general x1, matrix products, body(): jnp.einsum('qhd,khd->hqk', mixed_grad, value_heads, preferred_element_typ...  18 us
    convert_element_type x1, other arithmetic, body(): score_grad = (again_probs * (prob_grads - inner_sum)).astype(bf)  12.9 us
    dot_general x1, matrix products, body(): jnp.einsum('hqk,khd->qhd', jnp.exp(masked - log_total).astype(bf), value_...  11.8 us

profile of v2, /device:TPU:0, one launch (start us, length us, event | category | flops | bytes accessed | tf_op | source)
XLA Modules:
  0.0 509.6 jit_solution(5221521482952788881)
XLA Ops:
  2.3 4.8 concatenate.6
  10.1 37.8 %shard_map.349 = (bf16[2,2,2,2,2,24,768]{6,5,4,3,2,1,0:T(8,128)(2,1)S(1)}, bf16[2,2,2,2,2,24,768]{6,5,4,3,2,1,0:T(8,128)(2,1)S(1)}, bf16[2,2,2,2,2,24,768]{6,5,4...) custom-call(bf16[24,768]{1,0:T(8,128)(2,1)S(1)} %copy-done, ...), custom_call_target="tpu_custom_call" | custom-call | tf_op jit(solution)/shard_map/pallas_call | solution.py:86
  62.5 3.1 convolution_convert_fusion.4
  65.6 2.5 copy.79
  71.1 11.3 %fusion = (f32[12,576]{1,0:T(8,128)}, f32[12,576,576]{1,2,0:T(8,128)}) fusion(pred[576,576]{0,1:T(8,128)(4,1)S(1)} %fusion.45, bf16[576,12,64]{0,2,1:T(8,128)(2,1)} %bitcast.178, bf16[576,12,64]{0,2,1:T(8,128)(2,1)} %bitcast.176), kind=kOutput, calls=%fused_computation.5 | convolution fusion | flops 521544960 | bytes 18054144 | tf_op jit(solution)/shard_map/qhd,khd->hqk/dot_general | solution.py:601
  82.4 10.4 %exponential_reduce_fusion = f32[12,576]{1,0:T(8,128)} fusion(f32[12,576,576]{1,2,0:T(8,128)} %get-tuple-element.133, f32[12,576]{1,0:T(8,128)} %get-tuple-element.132, pred[576,576]{0,1:T(8,128)(4,1)} %copy-done.16), kind=kLoop, calls=%fused_computation.3 | loop fusion | flops 15918336 | bytes 16312320 | tf_op jit(solution)/shard_map/reduce_sum | solution.py:608
  95.6 3.1 add_convert_fusion.3
  98.7 2.4 copy.77
  101.1 11.8 %convolution_convert_fusion.2 = bf16[12,64,576]{2,1,0:T(8,128)(2,1)} fusion(bf16[576,12,64]{0,2,1:T(8,128)(2,1)} %bitcast.180, f32[12,576,576]{1,2,0:T(8,128)} %get-tuple-element.133, f32[12,576]{1,0:T(8,128)} %log_add_fusion, pred[576,576]{0,1:T(8,128)(4,1)} %copy-done.16), kind=kOutput, calls=%fused_computation.89 | convolution fusion | flops 525975552 | bytes 18054144 | tf_op jit(solution)/shard_map/hqk,khd->qhd/dot_general | solution.py:609
  113.6 2.9 fusion.118
  119.6 2.8 add_convert_fusion.1
  142.7 3.2 fusion.4
  145.9 3.7 fusion.2
  149.6 3.4 convolution_convert_fusion
  154.4 175.5 %shard_map.350 = (bf16[8,4,40,768]{3,2,1,0:T(8,128)(2,1)}, bf16[8,4,40,768]{3,2,1,0:T(8,128)(2,1)}, f32[4,768,768]{2,1,0:T(8,128)}, f32[4,1,768]{2,1,0:T(1,128)}, f32[4,768,768]{2,1,0:T(8,128)}) custom-call(bf16[8,4,40,768]{3,2,1,0:T(8,128)(2,1)} %bitcast.188, bf16[8,4,40,768]{3,2,1,0:T(8,128)(2,1)} %bitcast.187, bf16[4,768,3072]{2,1,0:T(8,128)(2,1)} %win_ref.1, ...), custom_call_target="tpu_custom_call" | custom-call | tf_op jit(solution)/shard_map/pallas_call | solution.py:447
  330.0 4.2 fusion.3
  334.2 2.6 fusion.6
  344.6 3.5 fusion.31
  352.4 3.4 fusion.33
  363.7 18.0 %multiply_reduce_fusion = (f32[12,576]{1,0:T(8,128)S(1)}, f32[12,576,576]{1,2,0:T(8,128)}) fusion(f32[12,576,576]{1,2,0:T(8,128)} %get-tuple-element.133, f32[12,576]{1,0:T(8,128)} %log_add_fusion, pred[576,576]{0,1:T(8,128)(4,1)} %copy-done.16, bf16[576,12,64]{0,2,1:T(8,128)(2,1)} %bitcast.182, bf16[576,12,64]{0,2,1:T(8,128)(2,1)} %bitcast.181), kind=kOutput, calls=%fused_computation.1 | convolution fusion | flops 529507584 | bytes 34007040 | tf_op jit(solution)/shard_map/qhd,khd->hqk/dot_general | solution.py:689
  381.8 12.9 %multiply_convert_fusion = bf16[12,576,576]{1,2,0:T(8,128)(2,1)S(1)} fusion(f32[12,576,576]{1,2,0:T(8,128)} %get-tuple-element.140, f32[12,576,576]{1,2,0:T(8,128)} %get-tuple-element.133, f32[12,576]{1,0:T(8,128)S(1)} %get-tuple-element.139, f32[12,576]{1,0:T(8,128)S(1)} %copy-done.39, pred[576,576]{0,1:T(8,128)(4,1)S(1)} %copy-done.17), kind=kLoop, calls=%fused_computation | loop fusion | flops 23887872 | bytes 40200192 | tf_op jit(solution)/shard_map/convert_element_type | solution.py:695
  394.7 2.7 multiply_convert_fusion.1
  403.5 10.6 %convert_reduce_fusion.1 = (f32[12,64]{1,0:T(8,128)S(1)}, bf16[12,64,576]{2,1,0:T(8,128)(2,1)S(1)}) fusion(bf16[576,12,64]{0,2,1:T(8,128)(2,1)S(1)} %bitcast.183, f32[12,576,576]{1,2,0:T(8,128)} %get-tuple-element.133, f32[12,576]{1,0:T(8,128)S(1)} %copy-done.39, pred[576,576]{0,1:T(8,128)(4,1)S(1)} %copy-done.17), kind=kOutput, calls=%fused_computation.34 | convolution fusion | flops 526859520 | bytes 18057216 | tf_op jit(solution)/shard_map/hqk,qhd->khd/dot_general | solution.py:690
  414.2 2.8 fusion.22
  418.7 4.0 fusion.53
  424.2 3.8 fusion.124.refs_2_
  428.0 2.5 fusion.123.refs_1_
  430.6 2.5 fusion.122.refs_0_
  433.1 2.5 fusion.54.refs_3_
  435.6 47.0 %shard_map.351 = (f32[24,768]{1,0:T(8,128)}, f32[24,768]{1,0:T(8,128)}, f32[24,768]{1,0:T(8,128)}, f32[24,768]{1,0:T(8,128)}, f32[16,128]{1,0:T(8,128)}) custom-call(f32[2,2,2,2,2,24,768]{6,5,4,3,2,1,0:T(8,128)} %fusion.122.refs_0_, f32[2,2,2,2,2,24,768]{6,5,4,3,2,1,0:T(8,128)} %fusion.123.refs_1_, f32[2,2,2,2,2,24,768]{6,5,4,3,2,1,0:T(8,128)} %fusion.124.refs_2_, ...), custom_call_target="tpu_custom_call" | custom-call | tf_op jit(solution)/shard_map/pallas_call | solution.py:186
  493.1 8.0 %copy.122 = f32[4,768,768]{2,1,0:T(8,128)} copy(f32[4,768,768]{2,1,0:T(8,128)} %get-tuple-element.180) | data formatting | bytes 18874368
  501.1 8.0 %copy.123 = f32[4,768,768]{2,1,0:T(8,128)} copy(f32[4,768,768]{2,1,0:T(8,128)} %get-tuple-element.182) | data formatting | bytes 18874368
  (253 shorter events, 89.9 us)
Async XLA Ops:
  54.6 3.7 copy-start.19
  54.6 3.7 copy-start.64
  54.6 3.7 copy-start.66
  54.6 3.7 copy-start.77
  71.1 11.3 %copy-start.16 = (pred[576,576]{0,1:T(8,128)(4,1)}, pred[576,576]{0,1:T(8,128)(4,1)S(1)}, u32[]{:S(2)}) copy-start(pred[576,576]{0,1:T(8,128)(4,1)S(1)} %fusion.45) | copy-start | bytes 995332
  116.4 6.0 %copy-start.40 = (f32[576]{0:T(1024)}, f32[576]{0:T(1024)S(1)}, u32[]{:S(2)}) copy-start(f32[576]{0:T(1024)S(1)} %broadcast_multiply_fusion.4) | copy-start | bytes 6916
  118.0 8.4 %copy-start.52 = (f32[576]{0:T(1024)}, f32[576]{0:T(1024)S(1)}, u32[]{:S(2)}) copy-start(f32[576]{0:T(1024)S(1)} %add_rsqrt_fusion) | copy-start | bytes 6916
  118.8 7.6 %copy-start.50 = (f32[768]{0:T(1024)}, f32[768]{0:T(1024)S(1)}, u32[]{:S(2)}) copy-start(f32[768]{0:T(1024)S(1)} %reshape.523) | copy-start | bytes 9220
  126.4 6.0 %copy-start.42 = (f32[576]{0:T(1024)}, f32[576]{0:T(1024)S(1)}, u32[]{:S(2)}) copy-start(f32[576]{0:T(1024)S(1)} %get-tuple-element.136) | copy-start | bytes 6916
  126.5 6.0 %copy-start.54 = (f32[576]{0:T(1024)}, f32[576]{0:T(1024)S(1)}, u32[]{:S(2)}) copy-start(f32[576]{0:T(1024)S(1)} %fusion.71) | copy-start | bytes 6916
  130.1 4.3 copy-start.11
  142.7 6.9 %copy-start.78 = (s32[576]{0:T(1024)}, s32[576]{0:T(1024)S(1)}, u32[]{:S(2)}) copy-start(s32[576]{0:T(1024)S(1)} %get-tuple-element.146) | copy-start | bytes 6916
  142.7 6.9 %copy-start.80 = (s32[576]{0:T(1024)}, s32[576]{0:T(1024)S(1)}, u32[]{:S(2)}) copy-start(s32[576]{0:T(1024)S(1)} %get-tuple-element.147) | copy-start | bytes 6916
  145.9 3.7 copy-start.23
  154.4 175.5 %copy-start.81 = (s32[576]{0:T(1024)S(1)}, s32[576]{0:T(1024)}, u32[]{:S(2)}) copy-start(s32[576]{0:T(1024)} %copy-done.80) | copy-start | bytes 6916
  329.9 4.3 copy-start.79
  329.9 4.3 copy-start.82
  344.6 3.5 copy-start.28
  344.6 3.5 copy-start.43
  344.6 3.5 copy-start.55
  344.6 4.7 copy-start.24
  363.7 18.0 %copy-start.17 = (pred[576,576]{0,1:T(8,128)(4,1)S(1)}, pred[576,576]{0,1:T(8,128)(4,1)}, u32[]{:S(2)}) copy-start(pred[576,576]{0,1:T(8,128)(4,1)} %copy-done.16) | copy-start | bytes 995332
  363.7 18.0 %copy-start.39 = (f32[12,576]{1,0:T(8,128)S(1)}, f32[12,576]{1,0:T(8,128)}, u32[]{:S(2)}) copy-start(f32[12,576]{1,0:T(8,128)} %log_add_fusion) | copy-start | bytes 82948
  381.8 12.9 %copy-start.18 = (bf16[576,768]{0,1:T(8,128)(2,1)S(1)}, bf16[576,768]{0,1:T(8,128)(2,1)}, u32[]{:S(2)}) copy-start(bf16[576,768]{0,1:T(8,128)(2,1)} %copy.78) | copy-start | bytes 2654212
  403.5 10.6 %copy-start.20 = (bf16[1,576,768]{2,1,0:T(8,128)(2,1)S(1)}, bf16[1,576,768]{2,1,0:T(8,128)(2,1)}, u32[]{:S(2)}) copy-start(bf16[1,576,768]{2,1,0:T(8,128)(2,1)} %param.22) | copy-start | bytes 2654212
  403.5 10.7 %copy-start.58 = (f32[576]{0:T(1024)S(1)}, f32[576]{0:T(1024)}, u32[]{:S(2)}) copy-start(f32[576]{0:T(1024)} %copy-done.57) | copy-start | bytes 6916
  403.5 10.7 %copy-start.65 = (f32[768]{0:T(1024)S(1)}, f32[768]{0:T(1024)}, u32[]{:S(2)}) copy-start(f32[768]{0:T(1024)} %reshape.518) | copy-start | bytes 9220
  403.5 10.7 %copy-start.69 = (f32[576]{0:T(1024)S(1)}, f32[576]{0:T(1024)}, u32[]{:S(2)}) copy-start(f32[576]{0:T(1024)} %copy-done.68) | copy-start | bytes 6916
  414.2 4.4 copy-start.10
  414.2 4.4 copy-start.67
  424.2 3.8 copy-start.33
  435.6 50.8 %copy-start.76 = (f32[4,1,768]{2,1,0:T(1,128)S(1)}, f32[4,1,768]{2,1,0:T(1,128)}, u32[]{:S(2)}) copy-start(f32[4,1,768]{2,1,0:T(1,128)} %get-tuple-element.46) | copy-start | bytes 36868
  (52 other events, 107.0 us)

commit v3 on v2

--- a/solution.py
+++ b/solution.py
@@ -194,65 +194,25 @@
     return outs[:count], outs[count]
 
 
-def pack_small(parts, lead):
-    flat = jnp.concatenate([p.reshape(lead + (-1,)) for p in parts], axis=-1)
-    size = flat.shape[-1]
-    room = -(-size // 2048) * 2048
-    flat = jnp.pad(flat, [(0, 0)] * len(lead) + [(0, room - size)])
-    return flat.reshape(lead + (room // 128, 128))
-
-
 def gather_all(vectors, weights, router, shift):
     axes = ("rep", "exp")
-    reps, groups = lax.axis_size("rep"), lax.axis_size("exp")
-    devices = reps * groups
-    per = weights[0].shape[0]
-    if per % 8 or devices & (devices - 1):
-        return (
-            [lax.all_gather(v, axes, axis=0, tiled=True) for v in vectors],
-            [lax.all_gather(w, axes, axis=0, tiled=True) for w in weights],
-            lax.all_gather(router, axes, axis=0, tiled=True),
-            lax.all_gather(shift, axes, axis=1, tiled=True),
-        )
-    small = pack_small(vectors + [router, shift], ())
-    weights, small = gather_params(weights, small, reps, groups)
-    small = small.reshape(devices, -1)
-    count = len(vectors)
-    got = [small[:, i * per : (i + 1) * per].reshape(-1) for i in range(count)]
-    at = count * per
-    wide = router.shape[1]
-    routers = small[:, at : at + per * wide].reshape(-1, wide)
-    at += per * wide
-    rows = shift.shape[0]
-    shifts = small[:, at : at + rows * per].reshape(devices, rows, per)
-    shifts = jnp.transpose(shifts, (1, 0, 2)).reshape(rows, -1)
-    return got, weights, routers, shifts
+    return (
+        [lax.all_gather(v, axes, axis=0, tiled=True) for v in vectors],
+        [lax.all_gather(w, axes, axis=0, tiled=True) for w in weights],
+        lax.all_gather(router, axes, axis=0, tiled=True),
+        lax.all_gather(shift, axes, axis=1, tiled=True),
+    )
 
 
 def scatter_all(vectors, weights, router, shift):
     axes = ("rep", "exp")
-    reps, groups = lax.axis_size("rep"), lax.axis_size("exp")
-    devices = reps * groups
-    per = weights[0].shape[0] // devices
-    if per % 8 or devices & (devices - 1):
-        return (
-            [lax.psum_scatter(v, axes, scatter_dimension=0, tiled=True) for v in vectors],
-            [lax.psum_scatter(w, axes, scatter_dimension=0, tiled=True) for w in weights],
-            lax.psum_scatter(router, axes, scatter_dimension=0, tiled=True),
-            lax.psum_scatter(shift, axes, scatter_dimension=1, tiled=True),
-        )
-    rows = shift.shape[0]
-    parted = jnp.transpose(shift.reshape(rows, devices, per), (1, 0, 2))
-    small = pack_small(vectors + [router, parted], (devices,))
-    weights, small = scatter_grads(weights, small, reps, groups)
-    small = small.reshape(-1)
-    count = len(vectors)
-    got = [small[i * per : (i + 1) * per] for i in range(count)]
-    at = count * per
-    wide = router.shape[1]
-    routers = small[at : at + per * wide].reshape(per, wide)
-    at += per * wide
-    return got, weights, routers, small[at : at + rows * per].reshape(rows, per)
+    return (
+        [lax.psum_scatter(v, axes, scatter_dimension=0, tiled=True) for v in vectors],
+        [lax.psum_scatter(w, axes, scatter_dimension=0, tiled=True) for w in weights],
+        lax.psum_scatter(router, axes, scatter_dimension=0, tiled=True),
+        lax.psum_scatter(shift, axes, scatter_dimension=1, tiled=True),
+    )
+
 
 def normal_parts(v):
     e = jnp.exp(v * v * -0.5)
@@ -534,7 +494,7 @@
     return ones, places
 
 
-def body(
+def body_plain(
     tokens,
     segments,
     valid,
@@ -648,15 +608,9 @@
         v = v.astype(bf).reshape(experts, room, feature_dim)
         return jnp.repeat(v, split, axis=0).reshape(groups, local_blocks, room, feature_dim)
 
-    small = reps == 4 and groups * room <= 512 and expert_in.shape[2] % (128 * reps) == 0
-    if small:
-        moved = experts_call(
-            outgoing(expert_slots), outgoing(sent), expert_in, expert_in_bias, expert_out, reps, groups
-        )
-    else:
-        moved = experts_plain(
-            outgoing(expert_slots), outgoing(sent), expert_in, expert_in_bias, expert_out
-        )
+    moved = experts_plain(
+        outgoing(expert_slots), outgoing(sent), expert_in, expert_in_bias, expert_out
+    )
     result, slot_back, in_w_grad, in_b_grad, out_w_grad = moved
     result = result.reshape(experts, split, room, feature_dim)
     slot_back = slot_back.reshape(experts, split, room, feature_dim)
@@ -744,6 +698,481 @@
     )
 
 
+def eye_of(n):
+    same = lax.broadcasted_iota(jnp.int32, (n, n), 0) == lax.broadcasted_iota(jnp.int32, (n, n), 1)
+    return same.astype(jnp.float32).astype(jnp.bfloat16)
+
+
+def lanes_of(n=1):
+    return lax.broadcasted_iota(jnp.int32, (n, 128), 1)
+
+
+def mask_of(ints, cols):
+    n = ints.shape[1]
+    same = lax.broadcasted_iota(jnp.int32, (n, n), 0) == lax.broadcasted_iota(jnp.int32, (n, n), 1)
+    near = cols[:, 0:1] == ints[0:1]
+    open_key = jnp.where(same, 1.0, cols[:, 1:2]) > 0
+    return jnp.where(near & open_key, 0.0, masked_score)
+
+
+def side_masks(head_dim):
+    lane = lanes_of()
+    return [
+        ((lane >= s * head_dim) & (lane < (s + 1) * head_dim)).astype(jnp.float32).astype(jnp.bfloat16)
+        for s in range(128 // head_dim)
+    ]
+
+
+def front_kernel(
+    capacity,
+    room,
+    head_dim,
+    tokens_ref,
+    cot_ref,
+    ints_ref,
+    small_ref,
+    wq_ref,
+    wk_ref,
+    wv_ref,
+    wo_ref,
+    xs_ref,
+    gs_ref,
+    resid_ref,
+    q_ref,
+    k_ref,
+    v_ref,
+    mixed_ref,
+    lse_ref,
+    info_ref,
+    mask_ref,
+    a2_ref,
+    sent_ref,
+):
+    f32, bf = jnp.float32, jnp.bfloat16
+    length, wide = tokens_ref.shape
+    groups, blocks = xs_ref.shape[:2]
+    ints = ints_ref[...]
+    eye = eye_of(length)
+    cols = dot(eye, ints.astype(bf), 1, 1)
+    rows = jnp.transpose(small_ref[...].astype(f32))
+    gain_one, bias_one, query_shift, value_shift, proj_shift, gain_two, bias_two = [
+        rows[64 + i : 65 + i] for i in range(7)
+    ]
+    inputs = tokens_ref[...].astype(f32)
+    unit_one, _ = normalize(inputs)
+    normed = (unit_one * gain_one + bias_one).astype(bf)
+    q_ref[...] = (dot(normed, wq_ref[...], 1, 0) + query_shift).astype(bf)
+    k_ref[...] = dot(normed, wk_ref[...], 1, 0).astype(bf)
+    v_ref[...] = (dot(normed, wv_ref[...], 1, 0) + value_shift).astype(bf)
+    mask_ref[...] = mask_of(ints, cols)
+    sides = side_masks(head_dim)
+    per = len(sides)
+    scale = jnp.full((1, 128), head_dim**-0.5, f32).astype(bf)
+
+    def heads(h, _):
+        at = pl.ds(pl.multiple_of(h * 128, 128), 128)
+        query = q_ref[:, at] * scale
+        total = jnp.zeros((128, length), f32)
+        for s, side in enumerate(sides):
+            score = dot(k_ref[:, at] * side, query, 1, 1) + mask_ref[...]
+            top = jnp.max(score, axis=0, keepdims=True)
+            expo = jnp.exp(score - top)
+            norm = jnp.sum(expo, axis=0, keepdims=True)
+            lse_ref[pl.ds(h * per + s, 1), :] = top + jnp.log(norm)
+            probs = (expo * (1.0 / norm)).astype(bf)
+            total = total + dot(v_ref[:, at] * side, probs, 0, 0)
+        mixed_ref[at, :] = total.astype(bf)
+        return 0
+
+    lax.fori_loop(0, wide // 128, heads, 0)
+    residual = inputs + dot(mixed_ref[...], wo_ref[...], 0, 0) + proj_shift
+    resid_ref[...] = residual
+    unit_two, _ = normalize(residual)
+    normed_two = (unit_two * gain_two + bias_two).astype(bf)
+    a2_ref[...] = normed_two
+    lane = lanes_of()
+    routed = (lane >= 32) & (lane < 64)
+    logits = jnp.where(routed, dot(normed_two, small_ref[...], 1, 0), masked_score)
+    logit_exp = jnp.exp(logits - jnp.max(logits, axis=1, keepdims=True))
+    probs = logit_exp / jnp.sum(logit_exp, axis=1, keepdims=True)
+    token_row = lax.broadcasted_iota(jnp.int32, (length, length), 1).astype(f32)
+    token_col = lax.broadcasted_iota(jnp.int32, (length, length), 0).astype(f32)
+    priority_row = ints[2:3] * 64.0 + ints[3:4]
+    priority_col = cols[:, 2:3] * 64.0 + cols[:, 3:4]
+    rank_col = jnp.sum(jnp.where(priority_row == token_col, token_row, 0.0), axis=1, keepdims=True)
+    rank_row = jnp.sum(jnp.where(priority_col == token_row, token_col, 0.0), axis=0, keepdims=True)
+    earlier = (rank_row < rank_col).astype(f32).astype(bf)
+    expert_lane = (lane - 32).astype(f32)
+    valid_col = cols[:, 1:2]
+    before = jnp.zeros((1, 128), f32)
+    info = probs
+    marks = jnp.zeros((length, 128), f32)
+    upstream = cot_ref[...].astype(f32)
+    for k in range(2):
+        expert = cols[:, 4 + k : 5 + k]
+        one = (expert == expert_lane).astype(f32)
+        live = one * valid_col
+        count = dot(earlier, live.astype(bf), 1, 0) + before
+        before = before + jnp.sum(live, axis=0, keepdims=True)
+        position = jnp.sum(count * one, axis=1, keepdims=True)
+        keep = valid_col * (position < capacity).astype(f32)
+        gate = jnp.sum(probs * one, axis=1, keepdims=True) * keep
+        place = jnp.where(keep > 0, expert * room + position, -1.0)
+        high = jnp.floor(place * (1.0 / 32.0))
+        low = place - high * 32.0
+        marks = jnp.where(lane == 2 * k, high, jnp.where(lane == 2 * k + 1, low, marks))
+        info = jnp.where(lane == k, place, jnp.where(lane == 2 + k, expert, info))
+        sent_ref[k] = (gate * upstream).astype(bf)
+    info_ref[...] = info
+    turned = dot(marks.astype(bf), eye, 0, 0)
+    place_rows = [turned[2 * k : 2 * k + 1] * 32.0 + turned[2 * k + 1 : 2 * k + 2] for k in range(2)]
+    part = blocks * room
+    slot = lax.broadcasted_iota(jnp.int32, (part, length), 0).astype(f32)
+
+    def fill(d, _):
+        first = (d * part).astype(f32)
+        hots = [(slot == row - first).astype(f32).astype(bf) for row in place_rows]
+        inside = dot(hots[0] + hots[1], a2_ref[...], 1, 0)
+        xs_ref[d] = inside.reshape(blocks, room, wide).astype(bf)
+        grads = dot(hots[0], sent_ref[0], 1, 0) + dot(hots[1], sent_ref[1], 1, 0)
+        gs_ref[d] = grads.reshape(blocks, room, wide).astype(bf)
+        return 0
+
+    lax.fori_loop(0, groups, fill, 0)
+
+
+def back_kernel(
+    head_dim,
+    tokens_ref,
+    cot_ref,
+    ints_ref,
+    small_ref,
+    wq_ref,
+    wk_ref,
+    wv_ref,
+    wo_ref,
+    res_ref,
+    ig_ref,
+    resid_ref,
+    q_ref,
+    k_ref,
+    v_ref,
+    mixed_ref,
+    lse_ref,
+    info_ref,
+    gin_ref,
+    gout_ref,
+    out_ref,
+    tokens_grad_ref,
+    wq_grad_ref,
+    wk_grad_ref,
+    wv_grad_ref,
+    wo_grad_ref,
+    small_grad_ref,
+    gin_out_ref,
+    gout_out_ref,
+    mask_ref,
+    mixed_grad_ref,
+    query_grad_ref,
+    key_grad_ref,
+    value_grad_ref,
+    gin_buf,
+    gout_buf,
+    sem,
+):
+    f32, bf = jnp.float32, jnp.bfloat16
+    length, wide = tokens_ref.shape
+    slots = res_ref.shape[0]
+    pieces = gin_ref.shape[0]
+    carried = ((gin_ref, gin_buf, gin_out_ref), (gout_ref, gout_buf, gout_out_ref))
+
+    def loads(j):
+        return [
+            pltpu.make_async_copy(src.at[j], buf, sem.at[0, i])
+            for i, (src, buf, _) in enumerate(carried)
+        ]
+
+    def stores(j):
+        return [
+            pltpu.make_async_copy(buf, dst.at[j], sem.at[1, i])
+            for i, (_, buf, dst) in enumerate(carried)
+        ]
+
+    for c in loads(0):
+        c.start()
+    ints = ints_ref[...]
+    cols = dot(eye_of(length), ints.astype(bf), 1, 1)
+    mask_ref[...] = mask_of(ints, cols)
+    small = small_ref[...]
+    rows = jnp.transpose(small.astype(f32))
+    gain_one, bias_one, _, _, _, gain_two, bias_two = [rows[64 + i : 65 + i] for i in range(7)]
+    lane = lanes_of()
+    routed = ((lane >= 32) & (lane < 64)).astype(f32)
+    info = info_ref[...]
+    probs = info * routed
+    upstream = cot_ref[...].astype(f32)
+    slot_row = lax.broadcasted_iota(jnp.int32, (1, slots), 1).astype(f32)
+    expert_lane = (lane - 32).astype(f32)
+    residual = resid_ref[...]
+    combined = residual
+    prob_grad = jnp.zeros((length, 128), f32)
+    gated = jnp.zeros((length, 128), f32)
+    hots = []
+    for k in range(2):
+        place, expert = info[:, k : k + 1], info[:, 2 + k : 3 + k]
+        kept = (expert == expert_lane).astype(f32) * (place >= 0).astype(f32)
+        gate = jnp.sum(probs * kept, axis=1, keepdims=True)
+        hot = (place == slot_row).astype(f32).astype(bf)
+        hots.append(hot)
+        picked = dot(hot, res_ref[...], 1, 0)
+        picked = picked + dot(pltpu.roll(kept, 96, 1).astype(bf), small, 1, 1)
+        combined = combined + gate * picked
+        prob_grad = prob_grad + kept * jnp.sum(upstream * picked, axis=1, keepdims=True)
+        gated = gated + kept * gate
+    out_ref[...] = combined.astype(bf)
+    inner = jnp.sum(probs * prob_grad, axis=1, keepdims=True)
+    logit_grad = (probs * (prob_grad - inner)).astype(bf)
+    unit_two, scale_two = normalize(residual)
+    normed_two = (unit_two * gain_two + bias_two).astype(bf)
+    high, low = two_parts(pltpu.roll(gated, 96, 1))
+    small_grad = dot(normed_two, logit_grad, 0, 0)
+    small_grad = small_grad + dot(cot_ref[...], high, 0, 0) + dot(cot_ref[...], low, 0, 0)
+    normed_two_grad = dot(hots[0] + hots[1], ig_ref[...], 1, 0) + dot(logit_grad, small, 1, 1)
+    vector_grads = {}
+    vector_grads[5] = jnp.sum(normed_two_grad * unit_two, axis=0, keepdims=True)
+    vector_grads[6] = jnp.sum(normed_two_grad, axis=0, keepdims=True)
+    residual_grad = upstream + normalize_back(normed_two_grad * gain_two, unit_two, scale_two)
+    tokens_grad_ref[...] = residual_grad
+    branch_grad = residual_grad.astype(bf)
+    wo_grad_ref[...] = dot(mixed_ref[...], branch_grad, 1, 0)
+    vector_grads[4] = jnp.sum(branch_grad.astype(f32), axis=0, keepdims=True)
+    mixed_grad_ref[...] = dot(branch_grad, wo_ref[...], 1, 1).astype(bf)
+    sides = side_masks(head_dim)
+    per = len(sides)
+    scale = jnp.full((1, 128), head_dim**-0.5, f32).astype(bf)
+
+    def heads(h, _):
+        at = pl.ds(pl.multiple_of(h * 128, 128), 128)
+        query = q_ref[:, at] * scale
+        mixed_grad = mixed_grad_ref[:, at]
+
+        @pl.when(h < pieces)
+        def _():
+            for c in loads(h):
+                c.wait()
+            for c in stores(h):
+                c.start()
+
+        query_total = jnp.zeros((128, length), f32)
+        key_total = jnp.zeros((length, 128), f32)
+        value_total = jnp.zeros((length, 128), f32)
+        for s, side in enumerate(sides):
+            key = k_ref[:, at] * side
+            score = dot(key, query, 1, 1) + mask_ref[...]
+            probs = jnp.exp(score - lse_ref[pl.ds(h * per + s, 1), :])
+            prob_grads = dot(v_ref[:, at] * side, mixed_grad, 1, 1)
+            inner = jnp.sum(probs * prob_grads, axis=0, keepdims=True)
+            score_grad = (probs * (prob_grads - inner)).astype(bf)
+            value_total = value_total + dot(probs.astype(bf), mixed_grad * side, 1, 0)
+            key_total = key_total + dot(score_grad, query * side, 1, 0)
+            query_total = query_total + dot(key * scale, score_grad, 0, 0)
+        @pl.when(h < pieces)
+        def _():
+            for c in stores(h):
+                c.wait()
+
+        @pl.when(h + 1 < pieces)
+        def _():
+            for c in loads(h + 1):
+                c.start()
+
+        query_grad_ref[:, at] = jnp.transpose(query_total).astype(bf)
+        key_grad_ref[:, at] = key_total.astype(bf)
+        value_grad_ref[:, at] = value_total.astype(bf)
+        return 0
+
+    lax.fori_loop(0, wide // 128, heads, 0)
+    inputs = tokens_ref[...].astype(f32)
+    unit_one, scale_one = normalize(inputs)
+    normed = (unit_one * gain_one + bias_one).astype(bf)
+    wq_grad_ref[...] = dot(normed, query_grad_ref[...], 0, 0)
+    wk_grad_ref[...] = dot(normed, key_grad_ref[...], 0, 0)
+    wv_grad_ref[...] = dot(normed, value_grad_ref[...], 0, 0)
+    vector_grads[2] = jnp.sum(query_grad_ref[...].astype(f32), axis=0, keepdims=True)
+    vector_grads[3] = jnp.sum(value_grad_ref[...].astype(f32), axis=0, keepdims=True)
+    normed_grad = dot(query_grad_ref[...], wq_ref[...], 1, 1)
+    normed_grad = normed_grad + dot(key_grad_ref[...], wk_ref[...], 1, 1)
+    normed_grad = normed_grad + dot(value_grad_ref[...], wv_ref[...], 1, 1)
+    vector_grads[0] = jnp.sum(normed_grad * unit_one, axis=0, keepdims=True)
+    vector_grads[1] = jnp.sum(normed_grad, axis=0, keepdims=True)
+    tokens_grad_ref[...] += normalize_back(normed_grad * gain_one, unit_one, scale_one)
+    line = lax.broadcasted_iota(jnp.int32, (128, wide), 0)
+    stacked = jnp.zeros((128, wide), f32)
+    for i in range(7):
+        stacked = jnp.where(line == 64 + i, vector_grads[i], stacked)
+    small_grad_ref[...] = small_grad + jnp.transpose(stacked)
+
+
+def front_call(capacity, room, groups, blocks, tokens, cot, ints, small, weights):
+    f32, bf = jnp.float32, jnp.bfloat16
+    length, wide = tokens.shape
+    shape = jax.ShapeDtypeStruct
+    vm = pl.BlockSpec(memory_space=pltpu.VMEM)
+    slots = shape((groups, blocks, room, wide), bf)
+    line = shape((length, wide), bf)
+    outs = [slots, slots, shape((length, wide), f32), line, line, line]
+    outs += [shape((wide, length), bf), shape((16, length), f32), shape((length, 128), f32)]
+    return pl.pallas_call(
+        functools.partial(front_kernel, capacity, room, wide // HEADS),
+        out_shape=outs,
+        in_specs=[vm] * 8,
+        out_specs=[vm] * len(outs),
+        scratch_shapes=[
+            pltpu.VMEM((length, length), f32),
+            pltpu.VMEM((length, wide), bf),
+            pltpu.VMEM((2, length, wide), bf),
+        ],
+        compiler_params=pltpu.CompilerParams(vmem_limit_bytes=60 * MIB),
+    )(tokens, cot, ints, small, *weights)
+
+
+def back_call(tokens, cot, ints, small, weights, res, ig, kept, gin, gout):
+    f32, bf = jnp.float32, jnp.bfloat16
+    length, wide = tokens.shape
+    shape = jax.ShapeDtypeStruct
+    vm = pl.BlockSpec(memory_space=pltpu.VMEM)
+    hbm = pl.BlockSpec(memory_space=pl.ANY)
+    square = shape((wide, wide), f32)
+    outs = [shape((length, wide), bf), shape((length, wide), f32)] + [square] * 4
+    outs += [shape((wide, 128), f32), shape(gin.shape, f32), shape(gout.shape, f32)]
+    line = pltpu.VMEM((length, wide), bf)
+    return pl.pallas_call(
+        functools.partial(back_kernel, wide // HEADS),
+        out_shape=outs,
+        in_specs=[vm] * 17 + [hbm] * 2,
+        out_specs=[vm] * 7 + [hbm] * 2,
+        scratch_shapes=[
+            pltpu.VMEM((length, length), f32),
+            line,
+            line,
+            line,
+            line,
+            pltpu.VMEM(gin.shape[1:], f32),
+            pltpu.VMEM(gout.shape[1:], f32),
+            pltpu.SemaphoreType.DMA((2, 2)),
+        ],
+        compiler_params=pltpu.CompilerParams(vmem_limit_bytes=60 * MIB),
+    )(tokens, cot, ints, small, *weights, res, ig, *kept, gin, gout)
+
+
+def body_fast(
+    tokens,
+    segments,
+    valid,
+    routes,
+    priority,
+    ln1_gain,
+    ln1_bias,
+    w_query,
+    query_bias,
+    w_key,
+    w_value,
+    value_bias,
+    w_attn_out,
+    attn_out_bias,
+    ln2_gain,
+    ln2_bias,
+    w_router,
+    expert_in,
+    expert_in_bias,
+    expert_out,
+    expert_out_bias,
+    cotangent,
+):
+    f32 = jnp.float32
+    reps, groups = lax.axis_size("rep"), lax.axis_size("exp")
+    devices = reps * groups
+    length, wide = tokens.shape[1:]
+    per = w_query.shape[0]
+    blocks = expert_in.shape[0]
+    capacity, room = capacity_of(routes.shape[2], length)
+    vectors = [ln1_gain, ln1_bias, query_bias, value_bias, attn_out_bias, ln2_gain, ln2_bias]
+    small = jnp.concatenate([expert_out_bias.T, w_router, jnp.stack(vectors, axis=1)], axis=1)
+    small = jnp.pad(small, ((0, 0), (0, 128 - small.shape[1])))
+    weights, small = gather_params([w_query, w_key, w_value, w_attn_out], small, reps, groups)
+    small = small.reshape(wide, 128)
+    first = priority[0]
+    ints = [segments[0], valid[0], first // 64, first % 64, routes[0, :, 0], routes[0, :, 1]]
+    ints = jnp.stack(ints + [first * 0] * 2).astype(f32)
+    xs, gs, *kept = front_call(
+        capacity, room, groups, blocks, tokens[0], cotangent[0], ints, small, weights
+    )
+    res, ig, gin, gb, gout = experts_call(
+        xs, gs, expert_in, expert_in_bias, expert_out, reps, groups
+    )
+    slots = groups * blocks * room
+    output, tokens_grad, *grads, small_grad, gin, gout = back_call(
+        tokens[0],
+        cotangent[0],
+        ints,
+        small,
+        weights,
+        res.reshape(slots, wide),
+        ig.reshape(slots, wide),
+        kept,
+        gin,
+        gout,
+    )
+    sums, last = scatter_grads(grads, small_grad.reshape(devices, per, 128), reps, groups)
+    columns = [last[:, 64 + i] for i in range(7)]
+    return (
+        output[None],
+        tokens_grad[None],
+        columns[0],
+        columns[1],
+        sums[0],
+        columns[2],
+        sums[1],
+        sums[2],
+        columns[3],
+        sums[3],
+        columns[4],
+        columns[5],
+        columns[6],
+        last[:, 32:64],
+        gin,
+        gb[:, 0],
+        gout,
+        last[:, :32].T,
+    )
+
+
+def capacity_of(top_count, length):
+    capacity = (105 * top_count * length + 100 * EXPERTS - 1) // (100 * EXPERTS)
+    return capacity, -(-capacity // 8) * 8
+
+
+def body(*args):
+    routes, w_query, expert_in = args[3], args[7], args[17]
+    reps, groups = lax.axis_size("rep"), lax.axis_size("exp")
+    _, room = capacity_of(routes.shape[2], routes.shape[1])
+    wide = w_query.shape[1]
+    suits = (
+        reps == 4
+        and groups & (groups - 1) == 0
+        and w_query.shape[0] % 8 == 0
+        and groups * room <= 512
+        and groups * expert_in.shape[0] == EXPERTS == 32
+        and expert_in.shape[2] % (128 * reps) == 0
+        and routes.shape[2] == 2
+        and routes.shape[1] <= 64 * 256
+        and 128 % (wide // HEADS) == 0
+        and HEADS <= 16
+        and expert_in.shape[0] < wide // 128
+    )
+    return body_fast(*args) if suits else body_plain(*args)
+
+
 def solution(mesh):
     in_specs = (
         P(("rep", "exp"), None, None),

time: 516 us -> 371 us (0.72)
  matrix products: 119 us -> 0 us
  Pallas kernels: 260 us -> 340 us
  local copies, waits for them, and re-layouts: 83.3 us -> 26.7 us
  other arithmetic: 45 us -> 2 us
    dot_general x33 -> x0, matrix products: 119 us -> none  [the longest x27 62.8 us: dot(): lax.dot_general(a, b, (((ca,), (cb,)), ((), ())), preferred_element_type=...]
    pallas_call x0 -> x2, Pallas kernels: none -> 79.3 us  [the longest x1 50.5 us: back_call(): pl.pallas_call(functools.partial(back_kernel, wide // HEADS), out_shape=o...]
    unnamed x180 -> x25, local copies, waits for them, and re-layouts: 36.8 us -> 14.5 us
    convert_element_type x11 -> x0, local copies, waits for them, and re-layouts: 17.4 us -> none  [the longest x7 7.84 us: body(): vectors = [v.astype(f32)[None] for v in vectors]]
    convert_element_type x6 -> x1, other arithmetic: 17.8 us -> 0.61 us  [body_fast(): ints = jnp.stack(ints + [first * 0] * 2).astype(f32)]
    reduce_sum x9 -> x0, other arithmetic: 16.5 us -> none  [the longest x1 10.4 us: body(): jnp.sum(jnp.exp(masked - top_score), axis=-1, keepdims=True)]
    reshape x18 -> x0, local copies, waits for them, and re-layouts: 13.5 us -> none  [the longest x11 5.18 us: pack_small(): flat = jnp.concatenate([p.reshape(lead + (-1,)) for p in parts], axis=-1)]
    another operation x0 -> x10, local copies, waits for them, and re-layouts: none -> 6.74 us  [the longest x7 5.23 us: body_fast(): jnp.stack(vectors, axis=1)]
where the time goes in v3:
time: 371 us; the launch traced here: 370 us
  Pallas kernels  340 us (92%)
  local copies, waits for them, and re-layouts  26.7 us (7%)
    pallas_call x1, Pallas kernels, experts_call(): pl.pallas_call(functools.partial(experts_kernel, reps, groups, compute),...  176 us
    pallas_call x1, Pallas kernels, back_call(): pl.pallas_call(functools.partial(back_kernel, wide // HEADS), out_shape=o...  50.5 us
    pallas_call x1, Pallas kernels, scatter_grads(): pl.pallas_call(functools.partial(scatter_kernel, dims, widths, count), ou...  47.6 us
    pallas_call x1, Pallas kernels, gather_params(): pl.pallas_call(functools.partial(gather_kernel, dims, widths, count), out...  37.9 us
    pallas_call x1, Pallas kernels, front_call(): pl.pallas_call(functools.partial(front_kernel, capacity, room, wide // HE...  28.8 us
    unnamed x25, local copies, waits for them, and re-layouts  14.5 us

profile of v3, /device:TPU:0, one launch (start us, length us, event | category | flops | bytes accessed | tf_op | source)
XLA Modules:
  0.0 369.8 jit_solution(15428324773799902500)
XLA Ops:
  0.7 0.8 slice_bitcast_fusion.1
  1.4 0.7 and_select_fusion
  2.1 0.7 and_select_fusion.1
  2.8 0.7 stack.30
  4.2 0.7 copy.47
  4.9 0.7 copy.48
  5.7 0.7 copy.49
  6.4 0.7 copy.50
  7.2 0.7 copy.51
  7.9 0.7 copy.52
  8.7 0.7 copy.53
  9.4 0.8 concatenate.3
  10.2 1.4 reshape.84.bias_ref
  11.6 0.8 copy-done.5
  12.4 0.8 copy-done.6
  13.2 0.8 copy-done.7
  14.0 0.8 copy-done.8
  14.7 37.9 %shard_map.349 = (bf16[2,2,2,2,2,24,768]{6,5,4,3,2,1,0:T(8,128)(2,1)S(1)}, bf16[2,2,2,2,2,24,768]{6,5,4,3,2,1,0:T(8,128)(2,1)S(1)}, bf16[2,2,2,2,2,24,768]{6,5,4...) custom-call(bf16[24,768]{1,0:T(8,128)(2,1)S(1)} %copy-done.5, ...), custom_call_target="tpu_custom_call" | custom-call | tf_op jit(solution)/shard_map/pallas_call | solution.py:86
  52.6 1.0 copy-done
  53.7 1.0 copy-done.1
  54.7 1.0 copy-done.2
  55.7 1.0 copy-done.3
  57.4 28.8 %shard_map.350 = (bf16[8,4,40,768]{3,2,1,0:T(8,128)(2,1)}, bf16[8,4,40,768]{3,2,1,0:T(8,128)(2,1)}, f32[576,768]{1,0:T(8,128)}, bf16[576,768]{1,0:T(8,128)(2,1)}...) custom-call(bf16[576,768]{1,0:T(8,128)(2,1)} %bitcast.43, ...), custom_call_target="tpu_custom_call" | custom-call | tf_op jit(solution)/shard_map/pallas_call | solution.py:1025
  86.2 175.6 %shard_map.351 = (bf16[8,4,40,768]{3,2,1,0:T(8,128)(2,1)}, bf16[8,4,40,768]{3,2,1,0:T(8,128)(2,1)}, f32[4,768,768]{2,1,0:T(8,128)}, f32[4,1,768]{2,1,0:T(1,128)}, f32[4,768,768]{2,1,0:T(8,128)}) custom-call(bf16[8,4,40,768]{3,2,1,0:T(8,128)(2,1)} %get-tuple-element.56.x_ref, bf16[8,4,40,768]{3,2,1,0:T(8,128)(2,1)} %get-tuple-element.57.g_ref, ...), custom_call_target="tpu_custom_call" | custom-call | tf_op jit(solution)/shard_map/pallas_call | solution.py:407
  261.8 50.5 %shard_map.352 = (bf16[576,768]{1,0:T(8,128)(2,1)}, f32[576,768]{1,0:T(8,128)}, f32[768,768]{1,0:T(8,128)}, f32[768,768]{1,0:T(8,128)}, f32[768,768]{1,0:T(8,128...) custom-call(bf16[576,768]{1,0:T(8,128)(2,1)} %bitcast.44, ...), custom_call_target="tpu_custom_call" | custom-call | tf_op jit(solution)/shard_map/pallas_call | solution.py:1049
  312.9 47.6 %shard_map.353 = (f32[24,768]{1,0:T(8,128)}, f32[24,768]{1,0:T(8,128)}, f32[24,768]{1,0:T(8,128)}, f32[24,768]{1,0:T(8,128)}, f32[24,128]{1,0:T(8,128)}) custom-call(f32[2,2,2,2,2,24,768]{6,5,4,3,2,1,0:T(8,128)} %bitcast.47, f32[2,2,2,2,2,24,768]{6,5,4,3,2,1,0:T(8,128)} %bitcast.48, f32[2,2,2,2,2,24,768]{6,5,4,3,2,1,0:T(8,128)} %bitcast.49, ...), custom_call_target="tpu_custom_call" | custom-call | tf_op jit(solution)/shard_map/pallas_call | solution.py:186
  360.4 1.8 slice_reduce_fusion
  362.2 1.5 slice_bitcast_fusion
  363.7 1.5 copy.61
  365.2 1.5 copy.62
  366.7 1.5 copy.63
  368.2 1.5 copy.64
  (16 shorter events, 1.9 us)
Async XLA Ops:
  11.6 0.8 copy-start.5
  12.4 0.8 copy-start.6
  13.2 0.8 copy-start.7
  13.9 0.8 copy-start.8
  52.6 1.0 copy-start
  53.7 1.0 copy-start.1
  54.7 1.0 copy-start.2
  55.7 1.0 copy-start.3
  56.7 0.7 copy-start.4
  261.8 50.5 %copy-start.9 = (f32[4,1,768]{2,1,0:T(1,128)S(1)}, f32[4,1,768]{2,1,0:T(1,128)}, u32[]{:S(2)}) copy-start(f32[4,1,768]{2,1,0:T(1,128)} %get-tuple-element.82) | copy-start | bytes 36868
